TPU v7x, 32 devices: a whole 2x2x4 slice. The times are simulated.
32 devices in a mesh: section: 2 (over core), tensor: 2 (over x), dp: 8 (over z, y).
Axes of the slice: x: 2, y: 2, z: 4, core: 2. Of those that a mesh axis runs over, the one named last changes fastest.
Arguments:
- byte_states: bfloat16 [32, 1024, 1024], P('dp'), may hold values from -6 to 6
- patch_ids: int32 [32, 1024], P('dp'), may hold values from 0 to 255, as said below
- attn_in: bfloat16 [2, 3, 1024, 1024], P('section', None, None, 'tensor'), may hold values from -0.1875 to 0.1875
- attn_out: bfloat16 [2, 1024, 1024], P('section', 'tensor'), may hold values from -0.5 to 0.5
- gains: float32 [2, 2, 1024], P('section'), may hold values from 0.1 to 1.9
- ffn_in: bfloat16 [1024, 2, 2816], P(None, None, 'tensor'), may hold values from -0.1875 to 0.1875
- ffn_out: bfloat16 [2816, 1024], P('tensor'), may hold values from -0.109375 to 0.109375
- latent_grad: bfloat16 [32, 256, 1024], P('dp'), may hold values from -6 to 6
Outputs:
- latents: bfloat16 [32, 256, 1024], P('dp', 'section', 'tensor')
- byte_grad: bfloat16 [32, 1024, 1024], P('dp', 'tensor', 'section')
- grad_attn_in: float32 [2, 3, 1024, 1024], P('section', None, None, 'tensor')
- grad_attn_out: float32 [2, 1024, 1024], P('section', 'tensor')
- grad_gains: float32 [2, 2, 1024], P('section')
- grad_ffn_in: float32 [1024, 2, 2816], P('section', None, 'tensor')
- grad_ffn_out: float32 [2816, 1024], P('tensor', 'section')
Inputs may be any that keep to these rules, and one draw needn't show every extreme that they name: `patch_ids`: in each sequence the ids start at 0 and rise by 0 or 1 from one byte to the next; a sequence has from 64 to 256 patches, and some sequence has exactly 256.
All inputs are finite; a program needn't handle non-finite values.
Results may differ from a plain program's by a relative error of at most 0.023.
Values may be sent and summed in bfloat16 or wider, within the bound.
A program may use at most 512 MiB of HBM per device.

v0:
```python
import jax
import jax.numpy as jnp
from jax import lax
from jax.sharding import PartitionSpec as P

HD = 64


EPSILON = 1e-05
NEGATIVE = -1000000000.0


def from_behind(value, axis, steps):
    count = lax.axis_size(axis)
    pairs = [(source, (source + steps) % count) for source in range(count)]
    return lax.ppermute(value, axis, pairs)


def partner(array, axis, apart):
    return lax.ppermute(array, axis, [(i, i ^ 1 << apart) for i in range(lax.axis_size(axis))])


def passed_along(array, axis, by):
    devices = lax.axis_size(axis)
    pairs = [(i, i + by) for i in range(devices) if 0 <= i + by < devices]
    return lax.ppermute(array, axis, pairs)


def normalize(values):
    return values * lax.rsqrt(jnp.mean(values * values, axis=-1, keepdims=True) + EPSILON)


def rms_norm(values, gain_row):
    return normalize(values) * gain_row


def norm_back(values, gain_row, upstream):
    _, pull_back = jax.vjp(lambda inner_values: rms_norm(inner_values, gain_row), values)
    return pull_back(upstream)[0]


def gain_grad(values, upstream):
    return jnp.sum(normalize(values) * upstream, axis=0)


def own_rows(values, index, count):
    return lax.dynamic_slice_in_dim(values, index * count, count, 0)


def split_heads(values):
    return values.reshape(values.shape[0], values.shape[1] // HD, HD).transpose(1, 0, 2)


def join_heads(values):
    return values.transpose(1, 0, 2).reshape(values.shape[1], values.shape[0] * values.shape[2])


def project(inputs, weight):
    return jnp.dot(inputs, weight, preferred_element_type=jnp.float32).astype(jnp.bfloat16)


def project_back(upstream, weight):
    return jnp.einsum("rc,dc->rd", upstream, weight, preferred_element_type=jnp.float32)


def weight_grad(inputs, upstream):
    return jnp.einsum("rd,rc->dc", inputs, upstream, preferred_element_type=jnp.float32)


def attend_forward(query_heads, key_heads, value_heads, allowed):
    head_count, row_count, _ = query_heads.shape
    block_rows = min(512, row_count)
    score_scale = HD ** (-0.5)

    def one_block(block_start):
        scores = (
            jnp.einsum("hqd,hkd->hqk", query_heads, key_heads, preferred_element_type=jnp.float32)
            * score_scale
        )
        scores = jnp.where(allowed(block_start, block_rows)[None], scores, NEGATIVE)
        highest = jnp.max(scores, axis=-1, keepdims=True)
        raised = jnp.exp(scores - highest)
        totals = jnp.sum(raised, axis=-1, keepdims=True)
        weights = (raised / totals).astype(jnp.bfloat16)
        mixed_out = jnp.einsum(
            "hqk,hkd->hqd", weights, value_heads, preferred_element_type=jnp.float32
        )
        return (mixed_out, (highest + jnp.log(totals))[..., 0])

    starts = jnp.arange(row_count // block_rows, dtype=jnp.int32) * block_rows
    mixed_out, log_totals = lax.map(one_block, starts)
    mixed_out = mixed_out.transpose(1, 0, 2, 3).reshape(head_count, row_count, HD)
    return (mixed_out, log_totals.transpose(1, 0, 2).reshape(head_count, row_count))


def attend_backward(query_heads, key_heads, value_heads, log_totals, grad_heads, allowed):
    head_count, row_count, _ = query_heads.shape
    block_rows = min(512, row_count)
    score_scale = HD ** (-0.5)

    def one_block(carried, block_start):
        key_grad, value_grad = carried
        scores = (
            jnp.einsum("hqd,hkd->hqk", query_heads, key_heads, preferred_element_type=jnp.float32)
            * score_scale
        )
        scores = jnp.where(allowed(block_start, block_rows)[None], scores, NEGATIVE)
        probs = jnp.exp(scores - log_totals[..., None])
        prob_grad = jnp.einsum(
            "hqd,hkd->hqk", grad_heads, value_heads, preferred_element_type=jnp.float32
        )
        deltas = jnp.sum(probs * prob_grad, axis=-1, keepdims=True)
        score_grad = (probs * (prob_grad - deltas)).astype(jnp.bfloat16)
        query_grad = (
            jnp.einsum("hqk,hkd->hqd", score_grad, key_heads, preferred_element_type=jnp.float32)
            * score_scale
        )
        key_grad = (
            key_grad
            + jnp.einsum(
                "hqk,hqd->hkd", score_grad, query_heads, preferred_element_type=jnp.float32
            )
            * score_scale
        )
        value_grad = value_grad + jnp.einsum(
            "hqk,hqd->hkd",
            probs.astype(jnp.bfloat16),
            grad_heads,
            preferred_element_type=jnp.float32,
        )
        return ((key_grad, value_grad), query_grad)

    zero_heads = jnp.zeros(key_heads.shape, jnp.float32)
    starts = jnp.arange(row_count // block_rows, dtype=jnp.int32) * block_rows
    (key_grad, value_grad), query_grad = lax.scan(one_block, (zero_heads, zero_heads), starts)
    query_grad = query_grad.transpose(1, 0, 2, 3).reshape(head_count, row_count, HD)
    return (query_grad, key_grad, value_grad)


def backward_projections(query_in, source_in, in_weights, grads):
    query_grad, key_grad, value_grad = [join_heads(piece).astype(jnp.bfloat16) for piece in grads]
    grad_in = jnp.stack(
        [
            weight_grad(query_in, query_grad),
            weight_grad(source_in, key_grad),
            weight_grad(source_in, value_grad),
        ]
    )
    query_back = project_back(query_grad, in_weights[0])
    source_back = project_back(key_grad, in_weights[1]) + project_back(value_grad, in_weights[2])
    return (query_back, source_back, grad_in)


def cross_forward(states16, ids_row, in_weights, layer_gains):
    byte_count = states16.shape[0]
    patch_count = byte_count // 4
    slot_ids = jnp.arange(patch_count, dtype=jnp.int32)
    states = states16.astype(jnp.float32)
    counts = jax.ops.segment_sum(
        jnp.ones((byte_count,), jnp.float32), ids_row, num_segments=patch_count
    )
    pooled = (
        jax.ops.segment_sum(states, ids_row, num_segments=patch_count)
        / jnp.maximum(counts, 1.0)[:, None]
    )
    row_valid = (slot_ids <= ids_row[byte_count - 1]).astype(jnp.float32)[:, None]
    query_in = rms_norm(pooled, layer_gains[0]).astype(jnp.bfloat16)
    source_in = rms_norm(states, layer_gains[1]).astype(jnp.bfloat16)
    projected = (
        project(query_in, in_weights[0]),
        project(source_in, in_weights[1]),
        project(source_in, in_weights[2]),
    )

    def member(block_start, block_rows):
        return ids_row[None, :] == (block_start + jnp.arange(block_rows, dtype=jnp.int32))[:, None]

    mixed_out, log_totals = attend_forward(
        split_heads(projected[0]), split_heads(projected[1]), split_heads(projected[2]), member
    )
    mixed16 = (join_heads(mixed_out) * row_valid).astype(jnp.bfloat16)
    return (pooled, counts, row_valid, query_in, source_in, projected, mixed16, log_totals, member)


def cross_backward(states16, ids_row, in_weights, out_weight, layer_gains, upstream16):
    pooled, counts, row_valid, query_in, source_in, projected, mixed16, log_totals, member = (
        cross_forward(states16, ids_row, in_weights, layer_gains)
    )
    grad_out = weight_grad(mixed16, upstream16)
    mixed_grad = (project_back(upstream16, out_weight) * row_valid).astype(jnp.bfloat16)
    grads = attend_backward(
        split_heads(projected[0]),
        split_heads(projected[1]),
        split_heads(projected[2]),
        log_totals,
        split_heads(mixed_grad),
        member,
    )
    query_back, source_back, grad_in = backward_projections(query_in, source_in, in_weights, grads)
    return (query_back, source_back, pooled, counts, grad_in, grad_out)


def latent_attention(latent, in_weights, gain_row):
    normed16 = rms_norm(latent, gain_row).astype(jnp.bfloat16)
    projected = (
        project(normed16, in_weights[0]),
        project(normed16, in_weights[1]),
        project(normed16, in_weights[2]),
    )
    slot_ids = jnp.arange(latent.shape[0], dtype=jnp.int32)

    def causal(block_start, block_rows):
        return slot_ids[None, :] <= (block_start + jnp.arange(block_rows, dtype=jnp.int32))[:, None]

    mixed_out, log_totals = attend_forward(
        split_heads(projected[0]), split_heads(projected[1]), split_heads(projected[2]), causal
    )
    return (normed16, projected, join_heads(mixed_out).astype(jnp.bfloat16), log_totals, causal)


def latent_attention_back(latent, in_weights, out_weight, gain_row, upstream16):
    normed16, projected, mixed16, log_totals, causal = latent_attention(
        latent, in_weights, gain_row
    )
    grad_out = weight_grad(mixed16, upstream16)
    mixed_grad = project_back(upstream16, out_weight).astype(jnp.bfloat16)
    grads = attend_backward(
        split_heads(projected[0]),
        split_heads(projected[1]),
        split_heads(projected[2]),
        log_totals,
        split_heads(mixed_grad),
        causal,
    )
    normed_back, source_back, grad_in = backward_projections(normed16, normed16, in_weights, grads)
    return (normed_back + source_back, grad_in, grad_out)


def ffn_forward(middle, ffn_in, gain_row):
    inner16 = rms_norm(middle, gain_row).astype(jnp.bfloat16)
    both = jnp.einsum("rd,dtf->rtf", inner16, ffn_in, preferred_element_type=jnp.float32)
    gate_value = both[:, 0, :]
    up_value = both[:, 1, :]
    hidden16 = (jax.nn.silu(gate_value) * up_value).astype(jnp.bfloat16)
    return (inner16, gate_value, up_value, hidden16)


def ffn_backward(middle, ffn_in, ffn_out, gain_row, upstream):
    inner16, gate_value, up_value, hidden16 = ffn_forward(middle, ffn_in, gain_row)
    upstream16 = upstream.astype(jnp.bfloat16)
    grad_down = weight_grad(hidden16, upstream16)
    hidden_grad = project_back(upstream16, ffn_out)
    _, pull_back = jax.vjp(
        lambda gate_in, up_in: jax.nn.silu(gate_in) * up_in, gate_value, up_value
    )
    gate_grad, up_grad = pull_back(hidden_grad)
    both_grad = jnp.stack([gate_grad, up_grad], axis=1).astype(jnp.bfloat16)
    grad_up = jnp.einsum("rd,rtf->dtf", inner16, both_grad, preferred_element_type=jnp.float32)
    inner_back = jnp.einsum("rtf,dtf->rd", both_grad, ffn_in, preferred_element_type=jnp.float32)
    return (inner_back, grad_up, grad_down)


def per_device(byte_states, patch_ids, attn_in, attn_out, gains, ffn_in, ffn_out, latent_grad):
    micro_count, byte_count, width = byte_states.shape
    patch_count = byte_count // 4
    column_count = attn_in.shape[-1]
    tensor_count = lax.axis_size("tensor")
    patch_share = patch_count // tensor_count
    byte_share = byte_count // tensor_count
    half_rows = patch_count // 2
    half_width = width // 2
    tensor_index = lax.axis_index("tensor")
    is_first = lax.axis_index("section") == 0
    in_weights = attn_in[0]
    out_weight = attn_out[0]
    layer_gains = gains[0]
    positions = jnp.arange(patch_count, dtype=jnp.int32)
    zero_patch = jnp.zeros((patch_count, width), jnp.float32)
    zero_bytes = jnp.zeros((byte_count, width), jnp.float32)
    zero_counts = jnp.zeros((patch_count,), jnp.float32)
    zero_in = jnp.zeros(in_weights.shape, jnp.float32)
    zero_out = jnp.zeros(out_weight.shape, jnp.float32)
    zero_up = jnp.zeros(ffn_in.shape, jnp.float32)
    zero_down = jnp.zeros(ffn_out.shape, jnp.float32)
    zero_gains = jnp.zeros((2, width), jnp.float32)
    zero_latent = jnp.zeros((patch_count, column_count), jnp.bfloat16)
    zero_byte_out = jnp.zeros((byte_share, width), jnp.bfloat16)
    zero_send = jnp.zeros((patch_count, width), jnp.bfloat16)
    in_total, out_total, up_total, down_total, gain_total = (
        zero_in,
        zero_out,
        zero_up,
        zero_down,
        zero_gains,
    )
    latent_parts = []
    byte_parts = []
    incoming = zero_send
    for tick in range(micro_count + 2):
        ahead = tick < micro_count
        middle = 1 <= tick <= micro_count
        behind = tick >= 2
        forward_index = min(tick, micro_count - 1)
        middle_index = min(max(tick - 1, 0), micro_count - 1)
        back_index = max(tick - 2, 0)
        received = incoming
        middle_valid = (positions <= patch_ids[middle_index][byte_count - 1]).astype(jnp.float32)[
            :, None
        ]
        upstream_full = latent_grad[middle_index].astype(jnp.float32) * middle_valid
        if tick <= micro_count:

            def first_one():
                if ahead:
                    kept = cross_forward(
                        byte_states[forward_index],
                        patch_ids[forward_index],
                        in_weights,
                        layer_gains,
                    )
                    return (
                        jnp.dot(kept[6], out_weight, preferred_element_type=jnp.float32),
                        kept[0],
                    )
                return (zero_patch, zero_patch)

            def second_one():
                if middle:
                    base_rows = received.astype(jnp.float32)
                    kept = latent_attention(base_rows, in_weights, layer_gains[0])
                    return (
                        jnp.dot(kept[2], out_weight, preferred_element_type=jnp.float32),
                        base_rows,
                    )
                return (zero_patch, zero_patch)

            head_part, residual = lax.cond(is_first, first_one, second_one)
            summed = residual + lax.psum(head_part, "tensor")
        else:
            residual = zero_patch
            summed = zero_patch
        if tick >= 1:

            def first_two():
                if behind:
                    return cross_backward(
                        byte_states[back_index],
                        patch_ids[back_index],
                        in_weights,
                        out_weight,
                        layer_gains,
                        received,
                    )
                return (zero_patch, zero_bytes, zero_patch, zero_counts, zero_in, zero_out)

            def second_two():
                if middle:
                    hidden16 = ffn_forward(summed, ffn_in, layer_gains[1])[3]
                    return (
                        jnp.dot(hidden16, ffn_out, preferred_element_type=jnp.float32),
                        zero_bytes,
                        zero_patch,
                        zero_counts,
                        zero_in,
                        zero_out,
                    )
                return (zero_patch, zero_bytes, zero_patch, zero_counts, zero_in, zero_out)

            mid_part, byte_part, pooled_old, counts_old, grad_in, grad_out = lax.cond(
                is_first, first_two, second_two
            )
            in_total = in_total + grad_in
            out_total = out_total + grad_out
            mid_sum = lax.psum(mid_part.astype(jnp.bfloat16), "tensor").astype(jnp.float32)
            if behind:
                byte_rows_sum = lax.psum_scatter(
                    byte_part.astype(jnp.bfloat16), "tensor", scatter_dimension=0, tiled=True
                ).astype(jnp.float32)
            else:
                byte_rows_sum = jnp.zeros((byte_share, width), jnp.float32)

            def first_three():
                if behind:
                    ids_own = own_rows(patch_ids[back_index], tensor_index, byte_share)
                    upstream = received.astype(jnp.float32)
                    pooled_grad = upstream + norm_back(pooled_old, layer_gains[0], mid_sum)
                    query_gain = gain_grad(
                        own_rows(pooled_old, tensor_index, patch_share),
                        own_rows(mid_sum, tensor_index, patch_share),
                    )
                    states_own = own_rows(byte_states[back_index], tensor_index, byte_share).astype(
                        jnp.float32
                    )
                    spread_back = (
                        jnp.take(pooled_grad, ids_own, axis=0)
                        / jnp.maximum(jnp.take(counts_old, ids_own), 1.0)[:, None]
                    )
                    byte_back = norm_back(states_own, layer_gains[1], byte_rows_sum) + spread_back
                    source_gain = gain_grad(states_own, byte_rows_sum)
                    return (
                        zero_patch,
                        zero_latent,
                        byte_back.astype(jnp.bfloat16),
                        zero_up,
                        zero_down,
                        jnp.stack([query_gain, source_gain]),
                    )
                return (zero_patch, zero_latent, zero_byte_out, zero_up, zero_down, zero_gains)

            def second_three():
                if middle:
                    output_rows = (summed + mid_sum) * middle_valid
                    latent16 = lax.dynamic_slice_in_dim(
                        output_rows, tensor_index * column_count, column_count, 1
                    ).astype(jnp.bfloat16)
                    inner_back, grad_up, grad_down = ffn_backward(
                        summed, ffn_in, ffn_out, layer_gains[1], upstream_full
                    )
                    return (inner_back, latent16, zero_byte_out, grad_up, grad_down, zero_gains)
                return (zero_patch, zero_latent, zero_byte_out, zero_up, zero_down, zero_gains)

            ffn_part, latent16, byte_out, grad_up, grad_down, gain_piece = lax.cond(
                is_first, first_three, second_three
            )
            up_total = up_total + grad_up
            down_total = down_total + grad_down
            gain_total = gain_total + gain_piece
            if middle:
                latent_parts.append(latent16)
            if behind:
                byte_parts.append(byte_out)
        if middle:
            ffn_share = lax.psum_scatter(
                ffn_part.astype(jnp.bfloat16), "tensor", scatter_dimension=0, tiled=True
            ).astype(jnp.float32)
            middle_own = own_rows(summed, tensor_index, patch_share)
            middle_grad = own_rows(upstream_full, tensor_index, patch_share) + norm_back(
                middle_own, layer_gains[1], ffn_share
            )
            ffn_gain = gain_grad(middle_own, ffn_share)
            branch_grad = lax.all_gather(
                middle_grad.astype(jnp.bfloat16), "tensor", axis=0, tiled=True
            )

            def first_five():
                return (zero_patch, zero_in, zero_out)

            def second_five():
                return latent_attention_back(
                    residual, in_weights, out_weight, layer_gains[0], branch_grad
                )

            attn_part, grad_in, grad_out = lax.cond(is_first, first_five, second_five)
            in_total = in_total + grad_in
            out_total = out_total + grad_out
            attn_share = lax.psum_scatter(
                attn_part.astype(jnp.bfloat16), "tensor", scatter_dimension=0, tiled=True
            ).astype(jnp.float32)
            residual_own = own_rows(residual, tensor_index, patch_share)
            input_grad = middle_grad + norm_back(residual_own, layer_gains[0], attn_share)
            attn_gain = gain_grad(residual_own, attn_share)
            second_only = jnp.where(is_first, 0.0, 1.0)
            gain_total = gain_total + jnp.stack([attn_gain, ffn_gain]) * second_only
            returned = lax.all_gather(input_grad.astype(jnp.bfloat16), "tensor", axis=0, tiled=True)
        else:
            returned = zero_send
        if tick <= micro_count:
            outgoing = jnp.where(is_first, summed.astype(jnp.bfloat16), returned)
            incoming = from_behind(outgoing, "section", 1)
    latents_local = jnp.stack(latent_parts)
    bytes_local = jnp.stack(byte_parts)
    send_latents = latents_local[:, :half_rows]
    send_bytes = bytes_local[:, :, half_width:]
    peer_latents, peer_bytes = partner((send_latents, send_bytes), "section", 0)
    latents = jnp.where(is_first, peer_latents, latents_local[:, half_rows:])
    byte_grad = jnp.where(is_first, bytes_local[:, :, :half_width], peer_bytes)
    gain_sum = lax.psum(gain_total, ("tensor", "dp"))
    in_sum, out_sum, up_sum, down_sum = (
        lax.psum(in_total.astype(jnp.bfloat16), "dp").astype(jnp.float32),
        lax.psum(out_total.astype(jnp.bfloat16), "dp").astype(jnp.float32),
        lax.psum(up_total.astype(jnp.bfloat16), "dp").astype(jnp.float32),
        lax.psum(down_total.astype(jnp.bfloat16), "dp").astype(jnp.float32),
    )
    moved_up, moved_down = (
        passed_along(up_sum[:half_width].astype(jnp.bfloat16), "section", -1).astype(jnp.float32),
        passed_along(down_sum[:, :half_width].astype(jnp.bfloat16), "section", -1).astype(
            jnp.float32
        ),
    )
    up_out = jnp.where(is_first, moved_up, up_sum[half_width:])
    down_out = jnp.where(is_first, moved_down, down_sum[:, half_width:])
    return (latents, byte_grad, in_sum[None], out_sum[None], gain_sum[None], up_out, down_out)


def solution(mesh):
    return jax.shard_map(
        per_device,
        mesh=mesh,
        in_specs=(
            P("dp", None, None),
            P("dp", None),
            P("section", None, None, "tensor"),
            P("section", "tensor", None),
            P("section", None, None),
            P(None, None, "tensor"),
            P("tensor", None),
            P("dp", None, None),
        ),
        out_specs=(
            P("dp", "section", "tensor"),
            P("dp", "tensor", "section"),
            P("section", None, None, "tensor"),
            P("section", "tensor", None),
            P("section", None, None),
            P("section", None, "tensor"),
            P("tensor", "section"),
        ),
        check_vma=False,
    )
```

profile of v0, /device:TPU:0, one launch (start us, length us, event | category | flops | bytes accessed | tf_op | source)
XLA Modules:
  0.0 2012.3 jit_solution(14713634159942415894)
XLA Ops:
  7.2 42.1 %conditional.19 = (f32[256,1024]{1,0:T(8,128)}, f32[256,1024]{1,0:T(8,128)}) conditional(s32[]{:T(128)} %convert_element_type.1303, () %tuple.229, (s32[4,1024]{1,0:T(4,128)}, bf16[4,1024,1024]{2,1,0:T(8,128)(2,1)}, f32[2,1024]{1,0:T(2,128)}, bf16[3,1024,512]{2,1,0:T(8,128)(2,1)}, bf16[512,1024]{1,0:T(8,128)(2,1)}) %tuple.484), branch_computations={%region_0.0_spmd, %region_1.8_spmd} | conditional | flops 3250720768 | bytes 79817336 | solution.py:337
  8.0 9.9 scatter_custom_fusion
  49.4 42.9 %all-reduce.13.cloned.1.call-done = f32[256,1024]{1,0:T(8,128)} async-done(((f32[256,1024]{1,0:T(8,128)}), f32[256,1024]{1,0:T(8,128)}) %all-reduce.13.cloned.1.call-update) | async-done | bytes 1048592 | tf_op jit(solution)/shard_map/psum | solution.py:338
  95.9 43.1 %conditional.20 = (f32[256,1024]{1,0:T(8,128)}, f32[256,1024]{1,0:T(8,128)S(1)}) conditional(s32[]{:T(128)} %convert_element_type.1303, (bf16[256,1024]{1,0:T(8,128)(2,1)S(1)}, f32[2,1024]{1,0:T(2,128)S(1)}, bf16[3,1024,512]{2,1,0:T(8,128)(2,1)}, bf16[512,1024]{1,0:T(8,128)(2,1)S(1)}) %tuple.486, (s32[4,1024]{1,0:T(4,128)S(1)}, ...), branch_computations={%region_9.13_spmd, %region_13.0_spmd} | conditional | flops 3250720768 | bytes 83978872 | solution.py:337
  96.1 9.9 scatter_custom_fusion.2
  141.0 38.2 %all-reduce.15.cloned.1.call-done = f32[256,1024]{1,0:T(8,128)} async-done(((f32[256,1024]{1,0:T(8,128)}), f32[256,1024]{1,0:T(8,128)}) %all-reduce.15.cloned.1.call-update) | async-done | bytes 1048592 | tf_op jit(solution)/shard_map/psum | solution.py:338
  190.1 28.0 %all-reduce.17.cloned.1.call-done = bf16[256,1024]{0,1:T(8,128)(2,1)} async-done(((bf16[256,1024]{0,1:T(8,128)(2,1)}), bf16[256,1024]{0,1:T(8,128)(2,1)}) %all-reduce.17.cloned.1.call-update) | async-done | bytes 524304 | tf_op jit(solution)/shard_map/psum | solution.py:374
  218.0 10.1 conditional.22
  228.3 33.4 %reduce-scatter.13.cloned.1.call-done = bf16[128,1024]{1,0:T(8,128)(2,1)} async-done(((bf16[256,1024]{1,0:T(8,128)(2,1)}), bf16[128,1024]{1,0:T(8,128)(2,1)}) %reduce-scatter.13.cloned.1.call-update) | async-done | bytes 262160 | tf_op jit(solution)/shard_map/reduce_scatter | solution.py:433
  264.8 8.8 all_gather.24
  280.0 46.7 %reduce-scatter.15.cloned.1.call-done = bf16[128,1024]{1,0:T(8,128)(2,1)} async-done(((bf16[256,1024]{1,0:T(8,128)(2,1)}), bf16[128,1024]{1,0:T(8,128)(2,1)}) %reduce-scatter.15.cloned.1.call-update) | async-done | bytes 262160 | tf_op jit(solution)/shard_map/reduce_scatter | solution.py:456
  340.7 43.6 %conditional.24 = (f32[256,1024]{1,0:T(8,128)}, f32[256,1024]{1,0:T(8,128)S(1)}) conditional(s32[]{:T(128)} %convert_element_type.1303, (bf16[256,1024]{1,0:T(8,128)(2,1)}, f32[2,1024]{1,0:T(2,128)S(1)}, bf16[3,1024,512]{2,1,0:T(8,128)(2,1)}, bf16[512,1024]{1,0:T(8,128)(2,1)S(1)}) %tuple.491, (s32[4,1024]{1,0:T(4,128)S(1)}, ...), branch_computations={%region_40.44_spmd, %region_44.0_spmd} | conditional | flops 3250720768 | bytes 83978872 | solution.py:337
  341.0 9.9 scatter_custom_fusion.4
  384.4 40.2 %all-reduce.19.cloned.1.call-done = f32[256,1024]{1,0:T(8,128)} async-done(((f32[256,1024]{1,0:T(8,128)}), f32[256,1024]{1,0:T(8,128)}) %all-reduce.19.cloned.1.call-update) | async-done | bytes 1048592 | tf_op jit(solution)/shard_map/psum | solution.py:338
  426.7 79.0 %conditional.25 = (bf16[256,1024]{1,0:T(8,128)(2,1)S(1)}, bf16[1024,1024]{1,0:T(8,128)(2,1)}, f32[256,1024]{1,0:T(8,128)}, f32[256]{0:T(256)S(1)}, f32[3,1024,512]{2,1,0:T(8,128)}, /*index=5*/f32[512,1024]{1,0:T(8,128)}) conditional(s32[]{:T(128)} %convert_element_type.1303, (f32[256,1024]{1,0:T(8,128)S(1)}, f32[2,1024]{1,0:T(2,128)S(1)}, ...), branch_computations={%region_52.54_spmd, %region_54.62_spmd} | conditional | flops 9464314880 | bytes 269960192 | solution.py:369
  426.7 10.7 scatter_custom_fusion.6
  508.0 27.3 %all-reduce.21.cloned.1.call-done = bf16[256,1024]{1,0:T(8,128)(2,1)} async-done(((bf16[256,1024]{1,0:T(8,128)(2,1)}), bf16[256,1024]{1,0:T(8,128)(2,1)}) %all-reduce.21.cloned.1.call-update) | async-done | bytes 524304 | tf_op jit(solution)/shard_map/psum | solution.py:374
  537.4 32.6 %reduce-scatter.17.cloned.1.call-done = bf16[512,1024]{1,0:T(8,128)(2,1)} async-done(((bf16[1024,1024]{1,0:T(8,128)(2,1)}), bf16[512,1024]{1,0:T(8,128)(2,1)}) %reduce-scatter.17.cloned.1.call-update) | async-done | bytes 1048592 | tf_op jit(solution)/shard_map/reduce_scatter | solution.py:376
  573.0 29.3 %conditional.26 = (bf16[256,1024]{1,0:T(8,128)(2,1)}, f32[1024,2,1408]{2,1,0:T(2,128)}, f32[1408,1024]{1,0:T(8,128)}, f32[2,1024]{1,0:T(2,128)S(1)}, bf16[1,256,...) conditional(s32[]{:T(128)} %convert_element_type.1303, (f32[256,1024]{1,0:T(8,128)}, ...), branch_computations={%region_64.66_spmd, %region_66.0_spmd} | conditional | flops 5919408128 | bytes 101611712 | solution.py:422
  602.5 14.5 reduce-scatter.19.cloned.1.call-done
  635.0 46.7 %reduce-scatter.21.cloned.1.call-done = bf16[128,1024]{1,0:T(8,128)(2,1)} async-done(((bf16[256,1024]{1,0:T(8,128)(2,1)}), bf16[128,1024]{1,0:T(8,128)(2,1)}) %reduce-scatter.21.cloned.1.call-update) | async-done | bytes 262160 | tf_op jit(solution)/shard_map/reduce_scatter | solution.py:456
  695.7 43.5 %conditional.28 = (f32[256,1024]{1,0:T(8,128)}, f32[256,1024]{1,0:T(8,128)S(1)}) conditional(s32[]{:T(128)} %convert_element_type.1303, (bf16[256,1024]{1,0:T(8,128)(2,1)}, f32[2,1024]{1,0:T(2,128)S(1)}, bf16[3,1024,512]{2,1,0:T(8,128)(2,1)}, bf16[512,1024]{1,0:T(8,128)(2,1)S(1)}) %tuple.498, (s32[4,1024]{1,0:T(4,128)S(1)}, ...), branch_computations={%region_86.92_spmd, %region_90.99_spmd} | conditional | flops 3250720768 | bytes 83978872 | solution.py:337
  696.2 9.9 scatter_custom_fusion.8
  739.3 40.2 %all-reduce.23.cloned.1.call-done = f32[256,1024]{1,0:T(8,128)} async-done(((f32[256,1024]{1,0:T(8,128)}), f32[256,1024]{1,0:T(8,128)}) %all-reduce.23.cloned.1.call-update) | async-done | bytes 1048592 | tf_op jit(solution)/shard_map/psum | solution.py:338
  781.6 79.2 %conditional.29 = (bf16[256,1024]{1,0:T(8,128)(2,1)S(1)}, bf16[1024,1024]{1,0:T(8,128)(2,1)}, f32[256,1024]{1,0:T(8,128)}, f32[256]{0:T(256)S(1)}, f32[3,1024,512]{2,1,0:T(8,128)}, /*index=5*/f32[512,1024]{1,0:T(8,128)}) conditional(s32[]{:T(128)} %convert_element_type.1303, (f32[256,1024]{1,0:T(8,128)S(1)}, f32[2,1024]{1,0:T(2,128)S(1)}, ...), branch_computations={%region_98.102_spmd, %region_100.110_spmd} | conditional | flops 9464314880 | bytes 269960192 | solution.py:369
  781.6 10.7 scatter_custom_fusion.10
  863.1 27.3 %all-reduce.25.cloned.1.call-done = bf16[256,1024]{1,0:T(8,128)(2,1)} async-done(((bf16[256,1024]{1,0:T(8,128)(2,1)}), bf16[256,1024]{1,0:T(8,128)(2,1)}) %all-reduce.25.cloned.1.call-update) | async-done | bytes 524304 | tf_op jit(solution)/shard_map/psum | solution.py:374
  892.6 32.5 %reduce-scatter.23.cloned.1.call-done = bf16[512,1024]{1,0:T(8,128)(2,1)} async-done(((bf16[1024,1024]{1,0:T(8,128)(2,1)}), bf16[512,1024]{1,0:T(8,128)(2,1)}) %reduce-scatter.23.cloned.1.call-update) | async-done | bytes 1048592 | tf_op jit(solution)/shard_map/reduce_scatter | solution.py:376
  928.1 29.1 %conditional.30 = (bf16[256,1024]{1,0:T(8,128)(2,1)}, f32[1024,2,1408]{2,1,0:T(2,128)}, f32[1408,1024]{1,0:T(8,128)}, f32[2,1024]{1,0:T(2,128)S(1)}, bf16[1,256,...) conditional(s32[]{:T(128)} %convert_element_type.1303, (f32[256,1024]{1,0:T(8,128)}, ...), branch_computations={%region_110.114_spmd, %region_112.122_spmd} | conditional | flops 5919408128 | bytes 101611712 | solution.py:422
  957.4 14.5 reduce-scatter.25.cloned.1.call-done
  975.0 8.8 all_gather.28
  990.2 46.7 %reduce-scatter.27.cloned.1.call-done = bf16[128,1024]{1,0:T(8,128)(2,1)} async-done(((bf16[256,1024]{1,0:T(8,128)(2,1)}), bf16[128,1024]{1,0:T(8,128)(2,1)}) %reduce-scatter.27.cloned.1.call-update) | async-done | bytes 262160 | tf_op jit(solution)/shard_map/reduce_scatter | solution.py:456
  1052.7 51.1 %all-reduce.27.cloned.1.call-done = f32[256,1024]{1,0:T(8,128)} async-done(((f32[256,1024]{1,0:T(8,128)}), f32[256,1024]{1,0:T(8,128)}) %all-reduce.27.cloned.1.call-update) | async-done | bytes 1048592 | tf_op jit(solution)/shard_map/psum | solution.py:338
  1105.9 78.7 %conditional.33 = (bf16[256,1024]{1,0:T(8,128)(2,1)S(1)}, bf16[1024,1024]{1,0:T(8,128)(2,1)}, f32[256,1024]{1,0:T(8,128)}, f32[256]{0:T(256)S(1)}, f32[3,1024,512]{2,1,0:T(8,128)}, /*index=5*/f32[512,1024]{1,0:T(8,128)}) conditional(s32[]{:T(128)} %convert_element_type.1303, (f32[256,1024]{1,0:T(8,128)S(1)}, f32[2,1024]{1,0:T(2,128)S(1)}, ...), branch_computations={%region_138.142_spmd, %region_140.150_spmd} | conditional | flops 9464314880 | bytes 269960192 | solution.py:369
  1105.9 10.7 scatter_custom_fusion.12
  1186.7 27.5 %all-reduce.29.cloned.1.call-done = bf16[256,1024]{1,0:T(8,128)(2,1)} async-done(((bf16[256,1024]{1,0:T(8,128)(2,1)}), bf16[256,1024]{1,0:T(8,128)(2,1)}) %all-reduce.29.cloned.1.call-update) | async-done | bytes 524304 | tf_op jit(solution)/shard_map/psum | solution.py:374
  1216.3 32.5 %reduce-scatter.29.cloned.1.call-done = bf16[512,1024]{1,0:T(8,128)(2,1)} async-done(((bf16[1024,1024]{1,0:T(8,128)(2,1)}), bf16[512,1024]{1,0:T(8,128)(2,1)}) %reduce-scatter.29.cloned.1.call-update) | async-done | bytes 1048592 | tf_op jit(solution)/shard_map/reduce_scatter | solution.py:376
  1251.8 29.2 %conditional.34 = (bf16[256,1024]{1,0:T(8,128)(2,1)}, f32[1024,2,1408]{2,1,0:T(2,128)}, f32[1408,1024]{1,0:T(8,128)}, f32[2,1024]{1,0:T(2,128)S(1)}, bf16[1,256,...) conditional(s32[]{:T(128)} %convert_element_type.1303, (f32[256,1024]{1,0:T(8,128)}, ...), branch_computations={%region_150.154_spmd, %region_152.162_spmd} | conditional | flops 5919408128 | bytes 101611712 | solution.py:422
  1281.2 14.5 reduce-scatter.31.cloned.1.call-done
  1314.0 46.7 %reduce-scatter.33.cloned.1.call-done = bf16[128,1024]{1,0:T(8,128)(2,1)} async-done(((bf16[256,1024]{1,0:T(8,128)(2,1)}), bf16[128,1024]{1,0:T(8,128)(2,1)}) %reduce-scatter.33.cloned.1.call-update) | async-done | bytes 262160 | tf_op jit(solution)/shard_map/reduce_scatter | solution.py:456
  1374.8 75.1 %conditional.36 = (f32[256,1024]{1,0:T(8,128)S(1)}, bf16[1024,1024]{1,0:T(8,128)(2,1)}, f32[256,1024]{1,0:T(8,128)S(1)}, f32[256]{0:T(256)S(1)}, f32[3,1024,512]{2,1,0:T(8,128)}, /*index=5*/f32[512,1024]{1,0:T(8,128)}) conditional(s32[]{:T(128)} %convert_element_type.1303, () %tuple.259, (s32[4,1024]{1,0:T(4,128)S(1)}, ...), branch_computations={%region_172.175_spmd, %region_173.183_spmd} | conditional | flops 9464314880 | bytes 272581696 | solution.py:369
  1375.0 10.8 scatter_custom_fusion.14
  1450.0 12.2 add_convert_fusion.2
  1462.2 22.1 %add_convert_fusion = bf16[1024,2,1408]{2,1,0:T(2,128)(2,1)} fusion(f32[1024,2,1408]{2,1,0:T(2,128)} %get-tuple-element.1200, f32[1024,2,1408]{2,1,0:T(2,128)} %get-tuple-element.1199, f32[1024,2,1408]{2,1,0:T(2,128)} %get-tuple-element.1339, f32[1024,2,1408]{2,1,0:T(2,128)} %get-tuple-element.1198), kind=kLoop, calls=%fused_computation.1052 | loop fusion | flops 11534336 | bytes 51904512 | tf_op jit(solution)/shard_map/convert_element_type | solution.py:481
  1485.2 20.0 fusion.628
  1523.7 15.7 conditional.37
  1544.6 383.0 %all-reduce.33.cloned.1.call-done = (bf16[1,3,1024,512]{3,2,1,0:T(8,128)(2,1)}, bf16[1,512,1024]{2,1,0:T(8,128)(2,1)}, bf16[1024,2,1408]{2,1,0:T(2,128)(2,1)}, bf16[1408,1024]{1,0:T(8,128)(2,1)}) async-done(((bf16[1,3,1024,512]{3,2,1,0:T(8,128)(2,1)}, bf16[1,512,1024]{2,1,0:T(8,128)(2,1)}, bf16[1024,2,1408]{2,1,0:T(2,128)(2,1)}, bf16[1408,1024]{1,0:T(8,128)(2,1)}), (bf16[1,3,1024,512]{3,2,1,0:T(8,128)(2,1)}, ...) | async-done | bytes 12845072 | tf_op jit(solution)/shard_map/psum | solution.py:479
  1945.2 40.0 %psum.117 = f32[1,2,1024]{2,1,0:T(2,128)} all-reduce(f32[1,2,1024]{2,1,0:T(2,128)S(1)} %fusion.682), channel_id=1, replica_groups=mesh['section'=2,'tensor'=2,'dp'=8] {'tensor','dp'}, use_global_device_ids=true, to_apply=%region_202.205 | all-reduce | flops 2048 | bytes 16384 | tf_op jit(solution)/shard_map/psum | solution.py:477
  (786 shorter events, 753.7 us)
Async XLA Ops:
  7.2 85.0 %all-reduce.13.cloned.1.call-start = ((), (), s32[]{:S(2)}) async-start(), calls=%async_computation.12 | async-start | bytes 2097152 | tf_op jit(solution)/shard_map/psum | solution.py:338
  49.3 46.6 %copy-start.12 = (bf16[1,512,1024]{2,1,0:T(8,128)(2,1)S(1)}, bf16[1,512,1024]{2,1,0:T(8,128)(2,1)}, u32[]{:S(2)}) copy-start(bf16[1,512,1024]{2,1,0:T(8,128)(2,1)} %param.53) | copy-start | bytes 3145732
  49.3 46.6 %copy-start.79 = (f32[1,2,1024]{2,1,0:T(2,128)S(1)}, f32[1,2,1024]{2,1,0:T(2,128)}, u32[]{:S(2)}) copy-start(f32[1,2,1024]{2,1,0:T(2,128)} %param.54) | copy-start | bytes 24580
  49.3 46.6 %copy-start.143 = (s32[4,1024]{1,0:T(4,128)S(1)}, s32[4,1024]{1,0:T(4,128)}, u32[]{:S(2)}) copy-start(s32[4,1024]{1,0:T(4,128)} %param.51) | copy-start | bytes 49156
  49.3 129.9 %all-reduce.15.cloned.1.call-start = ((), (), s32[]{:S(2)}) async-start(), calls=%async_computation.13 | async-start | bytes 2097152 | tf_op jit(solution)/shard_map/psum | solution.py:338
  93.9 2.0 collective-permute-start
  139.0 79.0 %all-reduce.17.cloned.1.call-start = ((), (), s32[]{:S(2)}) async-start(), calls=%async_computation.14 | async-start | bytes 1048576 | tf_op jit(solution)/shard_map/psum | solution.py:374
  184.3 77.5 %reduce-scatter.13.cloned.1.call-start = ((), (), s32[]{:S(2)}) async-start(), calls=%async_computation.15 | async-start | bytes 786432 | tf_op jit(solution)/shard_map/reduce_scatter | solution.py:433
  228.1 98.6 %reduce-scatter.15.cloned.1.call-start = ((), (), s32[]{:S(2)}) async-start(), calls=%async_computation.16 | async-start | bytes 786432 | tf_op jit(solution)/shard_map/reduce_scatter | solution.py:456
  228.2 100.2 %copy-start.140 = (f32[1,1,1024]{2,1,0:T(1,128)}, f32[1,1,1024]{2,1,0:T(1,128)S(1)}, u32[]{:S(2)}) copy-start(f32[1,1,1024]{2,1,0:T(1,128)S(1)} %get-tuple-element.1508) | copy-start | bytes 12292
  273.7 54.7 %copy-start.84 = (bf16[128,1024]{1,0:T(8,128)(2,1)S(1)}, bf16[128,1024]{1,0:T(8,128)(2,1)}, u32[]{:S(2)}) copy-start(bf16[128,1024]{1,0:T(8,128)(2,1)} %reduce-scatter.13.cloned.1.call-done) | copy-start | bytes 786436
  279.8 144.7 %all-reduce.19.cloned.1.call-start = ((), (), s32[]{:S(2)}) async-start(), calls=%async_computation.17 | async-start | bytes 2097152 | tf_op jit(solution)/shard_map/psum | solution.py:338
  338.6 2.1 collective-permute-start.1
  384.3 42.4 %copy-start.26 = (f32[256,1024]{1,0:T(8,128)}, f32[256,1024]{1,0:T(8,128)S(1)}, u32[]{:S(2)}) copy-start(f32[256,1024]{1,0:T(8,128)S(1)} %get-tuple-element.1142) | copy-start | bytes 3145732
  384.3 151.0 %all-reduce.21.cloned.1.call-start = ((), (), s32[]{:S(2)}) async-start(), calls=%async_computation.18 | async-start | bytes 1048576 | tf_op jit(solution)/shard_map/psum | solution.py:374
  506.5 63.5 %reduce-scatter.17.cloned.1.call-start = ((), (), s32[]{:S(2)}) async-start(), calls=%async_computation.19 | async-start | bytes 3145728 | tf_op jit(solution)/shard_map/reduce_scatter | solution.py:376
  507.3 109.8 %reduce-scatter.19.cloned.1.call-start = ((), (), s32[]{:S(2)}) async-start(), calls=%async_computation.20 | async-start | bytes 786432 | tf_op jit(solution)/shard_map/reduce_scatter | solution.py:433
  602.3 26.6 %copy-start.144 = (f32[2,1024]{1,0:T(2,128)}, f32[2,1024]{1,0:T(2,128)S(1)}, u32[]{:S(2)}) copy-start(f32[2,1024]{1,0:T(2,128)S(1)} %get-tuple-element.1193) | copy-start | bytes 24580
  602.3 79.3 %reduce-scatter.21.cloned.1.call-start = ((), (), s32[]{:S(2)}) async-start(), calls=%async_computation.21 | async-start | bytes 786432 | tf_op jit(solution)/shard_map/reduce_scatter | solution.py:456
  628.9 52.7 %copy-start.141 = (f32[1,1,1024]{2,1,0:T(1,128)S(1)}, f32[1,1,1024]{2,1,0:T(1,128)}, u32[]{:S(2)}) copy-start(f32[1,1,1024]{2,1,0:T(1,128)} %copy-done.140) | copy-start | bytes 12292
  628.9 54.5 %copy-start.86 = (bf16[128,1024]{1,0:T(8,128)(2,1)S(1)}, bf16[128,1024]{1,0:T(8,128)(2,1)}, u32[]{:S(2)}) copy-start(bf16[128,1024]{1,0:T(8,128)(2,1)} %reduce-scatter.19.cloned.1.call-done) | copy-start | bytes 786436
  634.8 144.7 %all-reduce.23.cloned.1.call-start = ((), (), s32[]{:S(2)}) async-start(), calls=%async_computation.22 | async-start | bytes 2097152 | tf_op jit(solution)/shard_map/psum | solution.py:338
  693.6 2.1 collective-permute-start.2
  739.3 42.4 %copy-start.30 = (f32[256,1024]{1,0:T(8,128)}, f32[256,1024]{1,0:T(8,128)S(1)}, u32[]{:S(2)}) copy-start(f32[256,1024]{1,0:T(8,128)S(1)} %get-tuple-element.1151) | copy-start | bytes 3145732
  739.3 151.2 %all-reduce.25.cloned.1.call-start = ((), (), s32[]{:S(2)}) async-start(), calls=%async_computation.23 | async-start | bytes 1048576 | tf_op jit(solution)/shard_map/psum | solution.py:374
  861.7 63.4 %reduce-scatter.23.cloned.1.call-start = ((), (), s32[]{:S(2)}) async-start(), calls=%async_computation.24 | async-start | bytes 3145728 | tf_op jit(solution)/shard_map/reduce_scatter | solution.py:376
  862.5 109.5 %reduce-scatter.25.cloned.1.call-start = ((), (), s32[]{:S(2)}) async-start(), calls=%async_computation.25 | async-start | bytes 786432 | tf_op jit(solution)/shard_map/reduce_scatter | solution.py:433
  957.2 26.6 %copy-start.146 = (f32[2,1024]{1,0:T(2,128)}, f32[2,1024]{1,0:T(2,128)S(1)}, u32[]{:S(2)}) copy-start(f32[2,1024]{1,0:T(2,128)S(1)} %get-tuple-element.1194) | copy-start | bytes 24580
  957.2 79.6 %reduce-scatter.27.cloned.1.call-start = ((), (), s32[]{:S(2)}) async-start(), calls=%async_computation.26 | async-start | bytes 786432 | tf_op jit(solution)/shard_map/reduce_scatter | solution.py:456
  983.8 53.1 %copy-start.142 = (f32[1,1,1024]{2,1,0:T(1,128)S(1)}, f32[1,1,1024]{2,1,0:T(1,128)}, u32[]{:S(2)}) copy-start(f32[1,1,1024]{2,1,0:T(1,128)} %copy-done.140) | copy-start | bytes 12292
  983.8 54.8 %copy-start.87 = (bf16[128,1024]{1,0:T(8,128)(2,1)S(1)}, bf16[128,1024]{1,0:T(8,128)(2,1)}, u32[]{:S(2)}) copy-start(bf16[128,1024]{1,0:T(8,128)(2,1)} %reduce-scatter.25.cloned.1.call-done) | copy-start | bytes 786436
  990.0 113.8 %all-reduce.27.cloned.1.call-start = ((), (), s32[]{:S(2)}) async-start(), calls=%async_computation.27 | async-start | bytes 2097152 | tf_op jit(solution)/shard_map/psum | solution.py:338
  1048.8 2.1 collective-permute-start.3
  1051.7 54.2 %copy-start.32 = (f32[256,1024]{1,0:T(8,128)}, f32[256,1024]{1,0:T(8,128)S(1)}, u32[]{:S(2)}) copy-start(f32[256,1024]{1,0:T(8,128)S(1)} %get-tuple-element.1160) | copy-start | bytes 3145732
  1052.6 161.6 %all-reduce.29.cloned.1.call-start = ((), (), s32[]{:S(2)}) async-start(), calls=%async_computation.28 | async-start | bytes 1048576 | tf_op jit(solution)/shard_map/psum | solution.py:374
  1185.4 63.4 %reduce-scatter.29.cloned.1.call-start = ((), (), s32[]{:S(2)}) async-start(), calls=%async_computation.29 | async-start | bytes 3145728 | tf_op jit(solution)/shard_map/reduce_scatter | solution.py:376
  1186.0 109.8 %reduce-scatter.31.cloned.1.call-start = ((), (), s32[]{:S(2)}) async-start(), calls=%async_computation.30 | async-start | bytes 786432 | tf_op jit(solution)/shard_map/reduce_scatter | solution.py:433
  1281.0 79.6 %reduce-scatter.33.cloned.1.call-start = ((), (), s32[]{:S(2)}) async-start(), calls=%async_computation.31 | async-start | bytes 786432 | tf_op jit(solution)/shard_map/reduce_scatter | solution.py:456
  1307.6 54.2 %copy-start.85 = (bf16[128,1024]{1,0:T(8,128)(2,1)S(1)}, bf16[128,1024]{1,0:T(8,128)(2,1)}, u32[]{:S(2)}) copy-start(bf16[128,1024]{1,0:T(8,128)(2,1)} %reduce-scatter.31.cloned.1.call-done) | copy-start | bytes 786436
  1313.8 207.1 %reduce-scatter.35.cloned.1.call-start = ((), (), s32[]{:S(2)}) async-start(), calls=%async_computation.33 | async-start | bytes 3145728 | tf_op jit(solution)/shard_map/reduce_scatter | solution.py:376
  1372.0 2.0 collective-permute-start.5
  1394.9 30.2 %copy-start.34 = (f32[256,1024]{1,0:T(8,128)}, f32[256,1024]{1,0:T(8,128)S(1)}, u32[]{:S(2)}) copy-start(f32[256,1024]{1,0:T(8,128)S(1)} %get-tuple-element.1646) | copy-start | bytes 3145732 | tf_op jit(solution)/shard_map/cond
  1449.9 73.7 %all-reduce.31.cloned.1.call-start = ((), (), s32[]{:S(2)}) async-start(), calls=%async_computation.32 | async-start | bytes 1048576 | tf_op jit(solution)/shard_map/psum | solution.py:374
  1485.2 442.5 %all-reduce.33.cloned.1.call-start = ((), (), s32[]{:S(2)}) async-start(), calls=%async_computation.34 | async-start | bytes 25690112 | tf_op jit(solution)/shard_map/psum | solution.py:479
  1544.6 440.6 %collective-permute-start.6 = (bf16[4,512,512]{2,1,0:T(8,128)(2,1)}, bf16[4,512,512]{2,1,0:T(8,128)(2,1)}, u32[]{:S(2)}, u32[]{:S(2)}) collective-permute-start(bf16[4,512,512]{2,1,0:T(8,128)(2,1)} %slice.601), channel_id=1, source_target_pairs={{0,16},{16,0},{1,17},{17,1},{2,18},{18,2},{3,19},{19,3},{4,20},{20... | collective-permute-start | bytes 6291464 | tf_op jit(solution)/shard_map/ppermute | solution.py:20
  1931.6 66.6 %collective-permute-start.7 = (bf16[512,2,1408]{2,1,0:T(2,128)(2,1)S(1)}, bf16[512,2,1408]{2,1,0:T(2,128)(2,1)}, u32[]{:S(2)}, u32[]{:S(2)}) collective-permute-start(bf16[512,2,1408]{2,1,0:T(2,128)(2,1)S(1)} %slice.602), channel_id=1, source_target_pairs={{16,0},{17,1},{18,2},{19,3},{20,4},{21,5},{22,6},{23,7},{24,8},{25... | collective-permute-start | bytes 8650760 | tf_op jit(solution)/shard_map/ppermute | solution.py:26
  1934.5 59.2 %collective-permute-start.8 = (bf16[1408,512]{1,0:T(8,128)(2,1)}, bf16[1408,512]{1,0:T(8,128)(2,1)}, u32[]{:S(2)}, u32[]{:S(2)}) collective-permute-start(bf16[1408,512]{1,0:T(8,128)(2,1)} %slice.604), channel_id=1, source_target_pairs={{16,0},{17,1},{18,2},{19,3},{20,4},{21,5},{22,6},{23,7},{24,8},{25... | collective-permute-start | bytes 4325384 | tf_op jit(solution)/shard_map/ppermute | solution.py:26
  1937.6 5.6 collective-permute-start.4
  (122 other events, 773.9 us)
Sparse Core Ops, SparseCore 0:
  49.4 42.7 all-reduce.12
  139.2 40.0 all-reduce.14
  184.4 33.5 all-reduce.16
  228.2 33.4 reduce-scatter.12
  279.9 46.7 reduce-scatter.14
  384.5 40.0 all-reduce.18
  506.7 28.5 all-reduce.20
  538.2 31.8 reduce-scatter.16
  602.5 14.5 reduce-scatter.18
  634.9 46.7 reduce-scatter.20
  739.4 40.0 all-reduce.22
  861.8 28.5 all-reduce.24
  893.3 31.8 reduce-scatter.22
  957.4 14.5 reduce-scatter.24
  990.1 46.7 reduce-scatter.26
  1052.8 50.9 all-reduce.26
  1185.5 28.6 all-reduce.28
  1217.0 31.8 reduce-scatter.28
  1281.2 14.5 reduce-scatter.30
  1313.9 46.6 reduce-scatter.32
  1450.0 31.8 reduce-scatter.34
  1485.3 28.5 all-reduce.30
  1519.2 408.3 all-reduce.32
where the time goes:
time: 2020 us; the launch traced here: 2010 us
  waiting for transfers between devices  1080 us (53%)
  other arithmetic  403 us (20%)
  matrix products  239 us (12%)
  local copies, waits for them, and re-layouts  148 us (7%)
  blocking collectives  110 us (5%)
    psum x1, waiting for transfers between devices, per_device(): lax.psum(in_total.astype(jnp.bfloat16), 'dp').astype(jnp.float32)  383 us
    psum x5, waiting for transfers between devices, per_device(): summed = residual + lax.psum(head_part, 'tensor')  212 us
    reduce_scatter x4, waiting for transfers between devices, per_device(): lax.psum_scatter(attn_part.astype(jnp.bfloat16), 'tensor', scatter_dimens...  187 us
    psum x5, waiting for transfers between devices, per_device(): lax.psum(mid_part.astype(jnp.bfloat16), 'tensor').astype(jnp.float32)  110 us
    reduce_scatter x4, waiting for transfers between devices, per_device(): lax.psum_scatter(byte_part.astype(jnp.bfloat16), 'tensor', scatter_dimens...  97.7 us
    scatter-add x8, other arithmetic, cross_forward(): jax.ops.segment_sum(states, ids_row, num_segments=patch_count)  82.5 us
    reduce_scatter x4, waiting for transfers between devices, per_device(): lax.psum_scatter(ffn_part.astype(jnp.bfloat16), 'tensor', scatter_dimensi...  77 us
    dot_general x24, matrix products, project(): jnp.dot(inputs, weight, preferred_element_type=jnp.float32)  76 us
  transfers between devices with their start and end apart: 32, of which 27 were waited for; matrix products, arithmetic and copies ran while one was open for 7% of the time, Pallas kernels for 0%

commit v1 on v0

v1 whole, which is shorter than its diff:
```python
import functools

import jax
import jax.numpy as jnp
from jax import lax
from jax.experimental import pallas as pl
from jax.experimental.pallas import tpu as pltpu
from jax.sharding import PartitionSpec as P

HD = 64
LANES = 128
BLOCK = 256
EPSILON = 1e-05
NEGATIVE = -1000000000.0
SCALE = HD ** (-0.5)
VMEM_BYTES = 56 * 1024 * 1024

f32 = jnp.float32
b16 = jnp.bfloat16


def dot(a, b):
    return jnp.dot(a, b, preferred_element_type=f32)


def dot_rt(a, b):
    return lax.dot_general(a, b, (((1,), (1,)), ((), ())), preferred_element_type=f32)


def dot_lt(a, b):
    return lax.dot_general(a, b, (((0,), (0,)), ((), ())), preferred_element_type=f32)


def inverse_rms(values):
    return lax.rsqrt(jnp.mean(values * values, axis=-1, keepdims=True) + EPSILON)


def norm_back(values, gain_row, upstream):
    inverse = inverse_rms(values)
    unit = values * inverse
    scaled = upstream * gain_row
    return (scaled - unit * jnp.mean(unit * scaled, axis=-1, keepdims=True)) * inverse, unit


def iota(shape, dim):
    return lax.broadcasted_iota(jnp.int32, shape, dim)


def one_hot(condition):
    return jnp.where(condition, 1.0, 0.0).astype(b16)


def head_sum(products, heads_in):
    high = products.astype(b16)
    low = (products - high.astype(f32)).astype(b16)
    return dot(high, heads_in) + dot(low, heads_in)


def spread_heads(small, heads_out):
    count, width = small.shape
    filled = jnp.concatenate([small, jnp.zeros((LANES - count, width), f32)], axis=0)
    return dot(filled.T.astype(b16), heads_out)


def scan_segments(values, ids, forward, combine, neutral):
    width = values.shape[1]
    lane = iota(ids.shape, 1)
    step = 1
    while step < width:
        shift = step if forward else width - step
        there = pltpu.roll(ids, shift, axis=1)
        inside = (lane >= step) if forward else (lane < width - step)
        same = jnp.logical_and(there == ids, inside)
        moved = pltpu.roll(values, shift, axis=1)
        values = combine(values, jnp.where(same, moved, neutral))
        step *= 2
    return values


def segment_max(values, ids):
    lowest = -3.0e38
    ahead = scan_segments(values, ids, True, jnp.maximum, lowest)
    return scan_segments(ahead, ids, False, jnp.maximum, lowest)


def segment_sum(values, ids):
    ahead = scan_segments(values, ids, True, jnp.add, 0.0)
    behind = scan_segments(values, ids, False, jnp.add, 0.0)
    return ahead + behind - values


def head_masks(width):
    heads_in = one_hot(iota((width, LANES), 0) // HD == iota((width, LANES), 1))
    heads_out = one_hot(iota((LANES, width), 1) // HD == iota((LANES, width), 0))
    return heads_in, heads_out


def each_block(count, body):
    @pl.loop(0, count // BLOCK)
    def _(index):
        body(pl.ds(pl.multiple_of(index * BLOCK, BLOCK), BLOCK))


def first_forward_kernel(
    states, id_row, id_col, wq, wk, wv, wo, gain,
    part, pooled, query_in, source_in, q, k, v, probs, mixed,
    pooled_sum, scores, mixed_sum,
):
    patches, width = pooled.shape
    byte_count = states.shape[0]
    columns = q.shape[1]
    heads = columns // HD
    heads_in, heads_out = head_masks(columns)
    pooled_sum[...] = jnp.zeros_like(pooled_sum)
    mixed_sum[...] = jnp.zeros_like(mixed_sum)

    def members(rows):
        return one_hot(iota((patches, BLOCK), 0) == id_row[:, rows])

    def project(rows):
        block = states[rows, :]
        pooled_sum[...] += dot(members(rows), block)
        values = block.astype(f32)
        normed = (values * inverse_rms(values) * gain[1:2, :]).astype(b16)
        source_in[rows, :] = normed
        k[rows, :] = dot(normed, wk[...]).astype(b16)
        v[rows, :] = dot(normed, wv[...]).astype(b16)

    each_block(byte_count, project)
    counts = jnp.sum(
        jnp.where(iota((patches, byte_count), 0) == id_row[...], 1.0, 0.0), axis=1, keepdims=True
    )
    pool = pooled_sum[...] / jnp.maximum(counts, 1.0)
    pooled[...] = pool
    normed_pool = (pool * inverse_rms(pool) * gain[0:1, :]).astype(b16)
    query_in[...] = normed_pool
    q[...] = dot(normed_pool, wq[...]).astype(b16)

    def score(rows):
        place = one_hot(id_col[rows, :] == iota((BLOCK, patches), 1))
        products = dot(place, q[...]) * k[rows, :].astype(f32)
        block_scores = head_sum(products, heads_in) * SCALE
        scores[:, rows] = block_scores.T[:heads, :]

    each_block(byte_count, score)
    ids = id_row[...]
    raised = jnp.exp(scores[...] - segment_max(scores[...], ids))
    probs[...] = raised / segment_sum(raised, ids)

    def mix(rows):
        weighted = spread_heads(probs[:, rows], heads_out) * v[rows, :].astype(f32)
        mixed_sum[...] += dot(members(rows), weighted.astype(b16))

    each_block(byte_count, mix)
    mixed16 = mixed_sum[...].astype(b16)
    mixed[...] = mixed16
    part[...] = dot(mixed16, wo[...]).astype(b16)


def second_attention_kernel(
    pooled, part_in, part_got, wq, wk, wv, wo, gain,
    latent, normed, q, k, v, totals, mixed, part,
):
    rows = pooled.shape[0]
    heads = q.shape[1] // HD
    latent16 = (pooled[...] + part_in[...].astype(f32) + part_got[...].astype(f32)).astype(b16)
    latent[...] = latent16
    values = latent16.astype(f32)
    normed16 = (values * inverse_rms(values) * gain[0:1, :]).astype(b16)
    normed[...] = normed16
    q[...] = dot(normed16, wq[...]).astype(b16)
    k[...] = dot(normed16, wk[...]).astype(b16)
    v[...] = dot(normed16, wv[...]).astype(b16)
    allowed = iota((rows, rows), 1) <= iota((rows, rows), 0)
    lane = iota((rows, LANES), 1)
    kept = jnp.zeros((rows, LANES), f32)
    outs = []
    for head in range(heads):
        own = slice(head * HD, (head + 1) * HD)
        scores = jnp.where(allowed, dot_rt(q[:, own], k[:, own]) * SCALE, NEGATIVE)
        highest = jnp.max(scores, axis=-1, keepdims=True)
        raised = jnp.exp(scores - highest)
        total = jnp.sum(raised, axis=-1, keepdims=True)
        outs.append(dot((raised / total).astype(b16), v[:, own]))
        kept = jnp.where(lane == head, highest + jnp.log(total), kept)
    totals[...] = kept
    mixed16 = jnp.concatenate(outs, axis=1).astype(b16)
    mixed[...] = mixed16
    part[...] = dot(mixed16, wo[...]).astype(b16)


def feed_forward_kernel(
    latent, part_in, part_got, upstream, gain, w_in, w_out,
    middle, inner, hidden, both_grad, out_part, inner_part,
    out_sum, inner_sum,
):
    step = pl.program_id(0)

    @pl.when(step == 0)
    def _():
        values = (
            latent[...].astype(f32) + part_in[...].astype(f32) + part_got[...].astype(f32)
        )
        middle[...] = values
        inner[...] = (values * inverse_rms(values) * gain[1:2, :]).astype(b16)
        out_sum[...] = jnp.zeros_like(out_sum)
        inner_sum[...] = jnp.zeros_like(inner_sum)

    both = dot(inner[...], w_in[...])
    gate = both[:, :LANES]
    up = both[:, LANES:]
    gated = 1.0 / (1.0 + jnp.exp(-gate))
    act = gate * gated
    hidden16 = (act * up).astype(b16)
    hidden[...] = hidden16
    out_sum[...] += dot(hidden16, w_out[...])
    hidden_grad = dot_rt(upstream[...], w_out[...])
    gate_grad = hidden_grad * up * (gated * (1.0 + gate * (1.0 - gated)))
    up_grad = hidden_grad * act
    grads = jnp.concatenate([gate_grad, up_grad], axis=1).astype(b16)
    both_grad[...] = grads
    inner_sum[...] += dot_rt(grads, w_in[...])

    @pl.when(step == pl.num_programs(0) - 1)
    def _():
        out_part[...] = out_sum[...]
        inner_part[...] = inner_sum[...].astype(b16)


def second_backward_kernel(
    middle, inner_part, inner_got, upstream, gain, q, k, v, totals, wq, wk, wv, wo,
    middle_grad, branch, dq, dk, dv, normed_part, gain_part,
):
    rows = middle.shape[0]
    heads = q.shape[1] // HD
    own_part = inner_part[...].astype(f32)
    back, unit = norm_back(middle[...], gain[1:2, :], own_part + inner_got[...].astype(f32))
    gain_part[...] = jnp.sum(unit * own_part, axis=0, keepdims=True)
    grad = upstream[...].astype(f32) + back
    middle_grad[...] = grad
    branch16 = grad.astype(b16)
    branch[...] = branch16
    mixed_grad = dot_rt(branch16, wo[...]).astype(b16)
    allowed = iota((rows, rows), 1) <= iota((rows, rows), 0)
    kept = totals[...]
    q_outs, k_outs, v_outs = [], [], []
    for head in range(heads):
        own = slice(head * HD, (head + 1) * HD)
        query, key, value, upper = q[:, own], k[:, own], v[:, own], mixed_grad[:, own]
        scores = jnp.where(allowed, dot_rt(query, key) * SCALE, NEGATIVE)
        probs = jnp.exp(scores - kept[:, head : head + 1])
        prob_grad = dot_rt(upper, value)
        delta = jnp.sum(probs * prob_grad, axis=-1, keepdims=True)
        score_grad = (probs * (prob_grad - delta)).astype(b16)
        q_outs.append(dot(score_grad, key) * SCALE)
        k_outs.append(dot_lt(score_grad, query) * SCALE)
        v_outs.append(dot_lt(probs.astype(b16), upper))
    q_grad = jnp.concatenate(q_outs, axis=1).astype(b16)
    k_grad = jnp.concatenate(k_outs, axis=1).astype(b16)
    v_grad = jnp.concatenate(v_outs, axis=1).astype(b16)
    dq[...] = q_grad
    dk[...] = k_grad
    dv[...] = v_grad
    normed_part[...] = (
        dot_rt(q_grad, wq[...]) + dot_rt(k_grad, wk[...]) + dot_rt(v_grad, wv[...])
    ).astype(b16)


def first_backward_kernel(
    latent, middle_grad, normed_part, normed_got, gain_up, gain, states, id_row, id_col, pooled,
    q, k, v, probs, wq, wk, wv, wo,
    branch, dq, dk, dv, query_part, source_part, gain_part,
    mixed_grad, scores, q_sum,
):
    patches, width = latent.shape
    byte_count = states.shape[0]
    columns = q.shape[1]
    heads = columns // HD
    heads_in, heads_out = head_masks(columns)
    own_part = normed_part[...].astype(f32)
    back, unit = norm_back(
        latent[...].astype(f32), gain_up[0:1, :], own_part + normed_got[...].astype(f32)
    )
    gain_part[0:1, :] = jnp.sum(unit * own_part, axis=0, keepdims=True)
    branch16 = (middle_grad[...] + back).astype(b16)
    branch[...] = branch16
    mixed_grad[...] = dot_rt(branch16, wo[...]).astype(b16)
    q_sum[...] = jnp.zeros_like(q_sum)

    def place(rows):
        return one_hot(id_col[rows, :] == iota((BLOCK, patches), 1))

    def value_side(rows):
        spread = dot(place(rows), mixed_grad[...])
        dv[rows, :] = (spread_heads(probs[:, rows], heads_out) * spread).astype(b16)
        sums = head_sum(spread * v[rows, :].astype(f32), heads_in)
        scores[:, rows] = sums.T[:heads, :]

    each_block(byte_count, value_side)
    ids = id_row[...]
    weights = probs[...]
    prob_grad = scores[...]
    scores[...] = weights * (prob_grad - segment_sum(weights * prob_grad, ids))
    gain_part[2:3, :] = jnp.zeros((1, width), f32)

    def key_side(rows):
        spread = spread_heads(scores[:, rows], heads_out)
        k_grad = (spread * dot(place(rows), q[...]) * SCALE).astype(b16)
        dk[rows, :] = k_grad
        members = one_hot(iota((patches, BLOCK), 0) == id_row[:, rows])
        q_sum[...] += dot(members, (spread * k[rows, :].astype(f32)).astype(b16))
        source = dot_rt(k_grad, wk[...]) + dot_rt(dv[rows, :], wv[...])
        source_part[rows, :] = source.astype(b16)
        values = states[rows, :].astype(f32)
        unit_block = values * inverse_rms(values)
        gain_part[2:3, :] += jnp.sum(unit_block * source, axis=0, keepdims=True)

    each_block(byte_count, key_side)
    q_grad = (q_sum[...] * SCALE).astype(b16)
    dq[...] = q_grad
    query = dot_rt(q_grad, wq[...])
    query_part[...] = query.astype(b16)
    pool = pooled[...]
    gain_part[1:2, :] = jnp.sum(pool * inverse_rms(pool) * query, axis=0, keepdims=True)


def byte_grad_kernel(
    branch, pooled, query_part, query_got, id_row, id_col, gain, states, source_part, source_got,
    out,
):
    patches, width = pooled.shape
    own_bytes = states.shape[0]
    byte_count = id_row.shape[1]
    query = query_part[...].astype(f32) + query_got[...].astype(f32)
    back, _ = norm_back(pooled[...], gain[0:1, :], query)
    counts = jnp.sum(
        jnp.where(iota((patches, byte_count), 0) == id_row[...], 1.0, 0.0), axis=1, keepdims=True
    )
    pool_grad = (branch[...].astype(f32) + back) / jnp.maximum(counts, 1.0)
    high = pool_grad.astype(b16)
    low = (pool_grad - high.astype(f32)).astype(b16)

    def finish(rows):
        place = one_hot(id_col[rows, :] == iota((BLOCK, patches), 1))
        spread = dot(place, high) + dot(place, low)
        source = source_part[rows, :].astype(f32) + source_got[rows, :].astype(f32)
        own, _ = norm_back(states[rows, :].astype(f32), gain[1:2, :], source)
        out[rows, :] = (own + spread).astype(b16)

    each_block(own_bytes, finish)


def shape(dims, dtype):
    return jax.ShapeDtypeStruct(dims, dtype)


def run(kernel, outs, args, scratch=(), flops=0):
    moved = sum(a.size * a.dtype.itemsize for a in args)
    moved += sum(o.size * o.dtype.itemsize for o in outs)
    whole = pl.BlockSpec(memory_space=pltpu.VMEM)
    return pl.pallas_call(
        kernel,
        out_shape=tuple(outs),
        in_specs=[whole] * len(args),
        out_specs=tuple([whole] * len(outs)),
        scratch_shapes=list(scratch),
        compiler_params=pltpu.CompilerParams(vmem_limit_bytes=VMEM_BYTES),
        cost_estimate=pl.CostEstimate(flops=flops, bytes_accessed=moved, transcendentals=0),
    )(*args)


def first_forward(states, ids, weights, w_out, gain):
    byte_count, width = states.shape
    patches = byte_count // 4
    columns = weights.shape[-1]
    heads = columns // HD
    outs = [
        shape((patches, width), b16),
        shape((patches, width), f32),
        shape((patches, width), b16),
        shape((byte_count, width), b16),
        shape((patches, columns), b16),
        shape((byte_count, columns), b16),
        shape((byte_count, columns), b16),
        shape((heads, byte_count), f32),
        shape((patches, columns), b16),
    ]
    scratch = [
        pltpu.VMEM((patches, width), f32),
        pltpu.VMEM((heads, byte_count), f32),
        pltpu.VMEM((patches, columns), f32),
    ]
    args = (states, ids[None, :], ids[:, None], weights[0], weights[1], weights[2], w_out, gain)
    flops = 2 * byte_count * width * columns * 3
    return run(first_forward_kernel, outs, args, scratch, flops)


def second_attention(pooled, part, got, weights, w_out, gain):
    patches, width = pooled.shape
    columns = weights.shape[-1]
    outs = [
        shape((patches, width), b16),
        shape((patches, width), b16),
        shape((patches, columns), b16),
        shape((patches, columns), b16),
        shape((patches, columns), b16),
        shape((patches, LANES), f32),
        shape((patches, columns), b16),
        shape((patches, width), b16),
    ]
    args = (pooled, part, got, weights[0], weights[1], weights[2], w_out, gain)
    return run(second_attention_kernel, outs, args, (), 2 * patches * width * columns * 6)


def feed_forward(latent, part, got, upstream, gain, w_in, w_out):
    patches, width = latent.shape
    hidden = w_out.shape[0]
    steps = hidden // LANES

    def fixed(dims):
        return pl.BlockSpec(dims, lambda i: (0, 0))

    rows = fixed((patches, width))
    outs = (
        shape((patches, width), f32),
        shape((patches, width), b16),
        shape((patches, hidden), b16),
        shape((patches, 2 * hidden), b16),
        shape((patches, width), f32),
        shape((patches, width), b16),
    )
    return pl.pallas_call(
        feed_forward_kernel,
        grid=(steps,),
        out_shape=outs,
        in_specs=[
            rows, rows, rows, rows, fixed(gain.shape),
            pl.BlockSpec((width, 2 * LANES), lambda i: (0, i)),
            pl.BlockSpec((LANES, width), lambda i: (i, 0)),
        ],
        out_specs=(
            rows, rows,
            pl.BlockSpec((patches, LANES), lambda i: (0, i)),
            pl.BlockSpec((patches, 2 * LANES), lambda i: (0, i)),
            rows, rows,
        ),
        scratch_shapes=[pltpu.VMEM((patches, width), f32), pltpu.VMEM((patches, width), f32)],
        compiler_params=pltpu.CompilerParams(
            vmem_limit_bytes=VMEM_BYTES, dimension_semantics=("arbitrary",)
        ),
        cost_estimate=pl.CostEstimate(
            flops=2 * patches * width * hidden * 6,
            bytes_accessed=hidden * width * 6 + patches * width * 40,
            transcendentals=0,
        ),
    )(latent, part, got, upstream, gain, w_in, w_out)


def second_backward(middle, part, got, upstream, gain, kept, weights, w_out):
    patches, width = middle.shape
    columns = weights.shape[-1]
    outs = [
        shape((patches, width), f32),
        shape((patches, width), b16),
        shape((patches, columns), b16),
        shape((patches, columns), b16),
        shape((patches, columns), b16),
        shape((patches, width), b16),
        shape((1, width), f32),
    ]
    args = (middle, part, got, upstream, gain, *kept, weights[0], weights[1], weights[2], w_out)
    return run(second_backward_kernel, outs, args, (), 2 * patches * width * columns * 6)


def first_backward(latent, middle_grad, part, got, gain_up, gain, states, ids, kept, weights, w_out):
    patches, width = latent.shape
    byte_count = states.shape[0]
    columns = weights.shape[-1]
    heads = columns // HD
    outs = [
        shape((patches, width), b16),
        shape((patches, columns), b16),
        shape((byte_count, columns), b16),
        shape((byte_count, columns), b16),
        shape((patches, width), b16),
        shape((byte_count, width), b16),
        shape((3, width), f32),
    ]
    scratch = [
        pltpu.VMEM((patches, columns), b16),
        pltpu.VMEM((heads, byte_count), f32),
        pltpu.VMEM((patches, columns), f32),
    ]
    pooled, q, k, v, probs = kept
    args = (
        latent, middle_grad, part, got, gain_up, gain, states, ids[None, :], ids[:, None], pooled,
        q, k, v, probs, weights[0], weights[1], weights[2], w_out,
    )
    flops = 2 * byte_count * width * columns * 3
    return run(first_backward_kernel, outs, args, scratch, flops)


def byte_gradient(branch, pooled, part, got, ids, own_ids, gain, states, source, source_got):
    args = (
        branch, pooled, part, got, ids[None, :], own_ids[:, None], gain, states, source, source_got,
    )
    (out,) = run(byte_grad_kernel, [shape(states.shape, b16)], args, (), 10**9)
    return out


def rows_at(values, start, count, axis=0):
    return lax.dynamic_slice_in_dim(values, start, count, axis)


def swap(values, axis):
    return lax.ppermute(values, axis, [(0, 1), (1, 0)])


def add(a, b):
    return (a.astype(f32) + b.astype(f32)).astype(b16)


def pick(values, index):
    return lax.dynamic_index_in_dim(values, index, 0, keepdims=False)


LONG, SHORT = 4, 2


class Grid:
    def __init__(self, sections):
        self.sections = sections
        place = lax.axis_index("dp")
        self.z = place // SHORT
        self.y = place % SHORT

    def send(self, values, moves):
        count = LONG * SHORT
        pairs = [(s * count + a, s * count + b) for s in self.sections for a, b in moves]
        return lax.ppermute(values, ("section", "dp"), pairs)

    def along(self, values, by, senders):
        moves = [
            (z * SHORT + y, (z + by) * SHORT + y) for z in senders for y in range(SHORT)
        ]
        return self.send(values, moves)

    def across(self, values):
        return self.send(values, [(i, i ^ 1) for i in range(LONG * SHORT)])

    def scatter_long(self, values):
        parts = values.reshape(LONG, -1, values.shape[-1])
        total = pick(parts, self.z)
        for by in (1, -1):
            running = pick(parts, (self.z - by) % LONG)
            for step in range(1, LONG):
                senders = range(0, step) if by > 0 else range(LONG - step, LONG)
                got = self.along(running, by, senders)
                if step < LONG - 1:
                    running = add(got, pick(parts, (self.z - by * (step + 1)) % LONG))
            total = add(total, got)
        return total

    def gather_long(self, value):
        full = jnp.zeros((LONG, *value.shape), value.dtype)
        full = lax.dynamic_update_index_in_dim(full, value, self.z, 0)
        for by in (1, -1):
            running = value
            for step in range(1, LONG):
                senders = range(step - 1, LONG - 1) if by > 0 else range(1, LONG - step + 1)
                running = self.along(running, by, senders)
                place = self.z - by * step
                inside = jnp.logical_and(place >= 0, place < LONG)
                spot = place % LONG
                current = pick(full, spot)
                full = lax.dynamic_update_index_in_dim(
                    full, jnp.where(inside, running, current), spot, 0
                )
        return full.reshape(-1, value.shape[-1])

    def scatter_short(self, values):
        parts = values.reshape(SHORT, -1, values.shape[-1])
        got = self.across(pick(parts, 1 - self.y))
        return add(got, pick(parts, self.y))

    def gather_short(self, value):
        got = self.across(value)
        low = jnp.where(self.y == 0, value, got)
        high = jnp.where(self.y == 0, got, value)
        return jnp.concatenate([low, high], axis=0)

    def long_first(self, values):
        mine = self.scatter_long(values)
        return self.gather_long(add(mine, self.across(mine)))

    def short_first(self, values):
        return self.gather_short(self.gather_long(self.scatter_long(self.scatter_short(values))))


def sum_over_groups(values, sections):
    if lax.axis_size("dp") == 1:
        return values
    if lax.axis_size("dp") != LONG * SHORT:
        return lax.psum(values, "dp")
    grid = Grid(sections)
    cut = values.shape[0] // 2
    return jnp.concatenate([grid.long_first(values[:cut]), grid.short_first(values[cut:])], axis=0)


def sum_small(values):
    values = values + swap(values, "tensor")
    values = values + swap(values, "section")
    if lax.axis_size("dp") != LONG * SHORT:
        return lax.psum(values, "dp")
    for apart in (1, 2, 4):
        values = values + lax.ppermute(
            values, "dp", [(i, i ^ apart) for i in range(LONG * SHORT)]
        )
    return values


def weight_grad(inputs, upstream):
    return jnp.einsum("rd,rc->dc", inputs, upstream, preferred_element_type=f32).astype(b16)


def per_device(byte_states, patch_ids, attn_in, attn_out, gains, ffn_in, ffn_out, latent_grad):
    sequences, byte_count, width = byte_states.shape
    patches = byte_count // 4
    columns = attn_in.shape[-1]
    hidden = ffn_out.shape[0]
    chunks = hidden // LANES
    own_count = sequences // 2
    own_bytes = byte_count // 2
    half_rows = patches // 2
    half_width = width // 2
    section = lax.axis_index("section")
    tensor = lax.axis_index("tensor")
    is_first = section == 0

    def both_layers(mine):
        other = swap(mine, "section")
        return jnp.where(is_first, mine, other), jnp.where(is_first, other, mine)

    first_in, second_in = both_layers(attn_in[0])
    first_out, second_out = both_layers(attn_out[0])
    first_gain, second_gain = both_layers(gains[0])
    w_in = ffn_in.reshape(width, 2, chunks, LANES).transpose(0, 2, 1, 3).reshape(width, 2 * hidden)
    w_out = ffn_out

    start = section * own_count
    states = [pick(byte_states, start + i) for i in range(own_count)]
    ids = [pick(patch_ids, start + i) for i in range(own_count)]
    valid = [
        (jnp.arange(patches, dtype=jnp.int32) <= row[byte_count - 1])[:, None] for row in ids
    ]
    upstream = [
        jnp.where(valid[i], pick(latent_grad, start + i), 0).astype(b16) for i in range(own_count)
    ]
    each = range(own_count)

    one = [first_forward(states[i], ids[i], first_in, first_out, first_gain) for i in each]
    got_one = [swap(one[i][0], "tensor") for i in each]
    two = [
        second_attention(one[i][1], one[i][0], got_one[i], second_in, second_out, second_gain)
        for i in each
    ]
    got_two = [swap(two[i][7], "tensor") for i in each]
    three = [
        feed_forward(two[i][0], two[i][7], got_two[i], upstream[i], second_gain, w_in, w_out)
        for i in each
    ]
    got_three = [swap(three[i][5], "tensor") for i in each]

    rows = lambda pieces: jnp.concatenate(pieces, axis=0)
    upstream_all = rows(upstream)
    hidden_all = rows([three[i][2] for i in each])
    inner_all = rows([three[i][1] for i in each])
    both_all = rows([three[i][3] for i in each])
    keep, give = section * half_width, (1 - section) * half_width
    down = add(
        weight_grad(hidden_all, rows_at(upstream_all, keep, half_width, 1)),
        swap(weight_grad(hidden_all, rows_at(upstream_all, give, half_width, 1)), "section"),
    )
    up = add(
        weight_grad(rows_at(inner_all, keep, half_width, 1), both_all),
        swap(weight_grad(rows_at(inner_all, give, half_width, 1), both_all), "section"),
    )
    down_sum = sum_over_groups(down, (0, 1))
    up_sum = sum_over_groups(up, (0, 1))

    four = [
        second_backward(
            three[i][0], three[i][5], got_three[i], upstream[i], second_gain,
            (two[i][2], two[i][3], two[i][4], two[i][5]), second_in, second_out,
        )
        for i in each
    ]
    got_four = [swap(four[i][5], "tensor") for i in each]

    def to_core(mine, source):
        return add(mine, lax.ppermute(mine, "section", [(source, 1 - source)]))

    second_grad_in = weight_grad(
        rows([two[i][1] for i in each]),
        rows([jnp.concatenate([four[i][2], four[i][3], four[i][4]], axis=1) for i in each]),
    )
    second_grad_out = weight_grad(rows([two[i][6] for i in each]), rows([four[i][1] for i in each]))
    second_in_sum = sum_over_groups(to_core(second_grad_in, 0), (1,))
    second_out_sum = sum_over_groups(to_core(second_grad_out, 0), (1,))

    five = [
        first_backward(
            two[i][0], four[i][0], four[i][5], got_four[i], second_gain, first_gain, states[i],
            ids[i], (one[i][1], one[i][4], one[i][5], one[i][6], one[i][7]), first_in, first_out,
        )
        for i in each
    ]
    source_all = rows([one[i][3] for i in each])
    first_grad_in = jnp.concatenate(
        [
            weight_grad(rows([one[i][2] for i in each]), rows([five[i][1] for i in each])),
            weight_grad(source_all, rows([five[i][2] for i in each])),
            weight_grad(source_all, rows([five[i][3] for i in each])),
        ],
        axis=1,
    )
    first_grad_out = weight_grad(rows([one[i][8] for i in each]), rows([five[i][0] for i in each]))
    first_in_sum = sum_over_groups(to_core(first_grad_in, 1), (0,))
    first_out_sum = sum_over_groups(to_core(first_grad_out, 1), (0,))

    byte_start, byte_other = tensor * own_bytes, (1 - tensor) * own_bytes
    finished = []
    for i in each:
        query_got = swap(five[i][4], "tensor")
        source_got = swap(rows_at(five[i][5], byte_other, own_bytes), "tensor")
        finished.append(
            byte_gradient(
                five[i][0], one[i][1], five[i][4], query_got, ids[i],
                rows_at(ids[i], byte_start, own_bytes), first_gain,
                rows_at(states[i], byte_start, own_bytes),
                rows_at(five[i][5], byte_start, own_bytes), source_got,
            )
        )
    byte_own = jnp.stack(finished)
    byte_keep = rows_at(byte_own, keep, half_width, 2)
    byte_got = swap(rows_at(byte_own, give, half_width, 2), "section")
    byte_grad = jnp.where(
        is_first,
        jnp.concatenate([byte_keep, byte_got]),
        jnp.concatenate([byte_got, byte_keep]),
    )

    latent_parts = []
    mine, theirs = tensor * columns, (1 - tensor) * columns
    for i in each:
        total = three[i][4]
        got = swap(rows_at(total, theirs, columns, 1).astype(b16), "tensor")
        value = rows_at(three[i][0] + total, mine, columns, 1) + got.astype(f32)
        latent_parts.append(jnp.where(valid[i], value, 0.0).astype(b16))
    latent_own = jnp.stack(latent_parts)
    latent_keep = rows_at(latent_own, section * half_rows, half_rows, 1)
    latent_got = swap(rows_at(latent_own, (1 - section) * half_rows, half_rows, 1), "section")
    latents = jnp.where(
        is_first,
        jnp.concatenate([latent_keep, latent_got]),
        jnp.concatenate([latent_got, latent_keep]),
    )

    gain_rows = sum(
        jnp.concatenate([five[i][6][1:3], five[i][6][0:1], four[i][6]], axis=0) for i in each
    )
    gain_sum = sum_small(gain_rows)
    gain_out = jnp.where(is_first, gain_sum[0:2], gain_sum[2:4])
    in_sum = jnp.where(is_first, first_in_sum, second_in_sum).astype(f32)
    in_out = in_sum.reshape(width, 3, columns).transpose(1, 0, 2)
    out_out = jnp.where(is_first, first_out_sum, second_out_sum).astype(f32)
    up_out = (
        up_sum.astype(f32).reshape(half_width, chunks, 2, LANES).transpose(0, 2, 1, 3)
    ).reshape(half_width, 2, hidden)
    down_out = down_sum.astype(f32)
    return (latents, byte_grad, in_out[None], out_out[None], gain_out[None], up_out, down_out)


def solution(mesh):
    return jax.shard_map(
        per_device,
        mesh=mesh,
        in_specs=(
            P("dp", None, None),
            P("dp", None),
            P("section", None, None, "tensor"),
            P("section", "tensor", None),
            P("section", None, None),
            P(None, None, "tensor"),
            P("tensor", None),
            P("dp", None, None),
        ),
        out_specs=(
            P("dp", "section", "tensor"),
            P("dp", "tensor", "section"),
            P("section", None, None, "tensor"),
            P("section", "tensor", None),
            P("section", None, None),
            P("section", None, "tensor"),
            P("tensor", "section"),
        ),
        check_vma=False,
    )
```

time: 2020 us -> 1300 us (0.64)
  waiting for transfers between devices: 1080 us -> 105 us
  starting transfers between devices: 7.82 us -> 417 us
  local copies, waits for them, and re-layouts: 148 us -> 468 us
  other arithmetic: 403 us -> 109 us
  matrix products: 239 us -> 25 us
  Pallas kernels: 0 us -> 146 us
  blocking collectives: 110 us -> 0 us
    psum x11 -> x0, waiting for transfers between devices: 706 us -> none  [the longest x1 383 us: per_device(): lax.psum(in_total.astype(jnp.bfloat16), 'dp').astype(jnp.float32)]
    ppermute x9 -> x192, starting transfers between devices: 6.88 us -> 417 us  [the longest x162 312 us: send(): return lax.ppermute(values, ('section', 'dp'), pairs)]
    reduce_scatter x12 -> x0, waiting for transfers between devices: 361 us -> none  [the longest x4 187 us: per_device(): lax.psum_scatter(attn_part.astype(jnp.bfloat16), 'tensor', scatter_dimens...]
    dynamic_update_slice x0 -> x14, local copies, waits for them, and re-layouts: none -> 244 us  [the longest x12 208 us: gather_long(): lax.dynamic_update_index_in_dim(full, jnp.where(inside, running, current)...]
    dot_general x88 -> x10, matrix products: 211 us -> 25 us  [weight_grad(): jnp.einsum('rd,rc->dc', inputs, upstream, preferred_element_type=f32)]
    pallas_call x0 -> x12, Pallas kernels: none -> 146 us  [the longest x10 107 us: run(): pl.pallas_call(kernel, out_shape=tuple(outs), in_specs=[whole] * len(args...]
    scatter-add x16 -> x0, other arithmetic: 144 us -> none  [the longest x8 82.5 us: cross_forward(): jax.ops.segment_sum(states, ids_row, num_segments=patch_count)]
    ppermute x9 -> x192, waiting for transfers between devices: 11.6 us -> 105 us  [the longest x162 78.1 us: send(): return lax.ppermute(values, ('section', 'dp'), pairs)]
  transfers between devices with their start and end apart: 32 -> 192, of which waited for: 27 -> 35; matrix products, arithmetic and copies ran while one was open for 7% -> 43% of each run, Pallas kernels for 0% -> 10%
where the time goes in v1:
time: 1300 us; the launch traced here: 1270 us
  local copies, waits for them, and re-layouts  468 us (36%)
  starting transfers between devices  417 us (32%)
  Pallas kernels  146 us (11%)
  other arithmetic  109 us (8%)
  waiting for transfers between devices  105 us (8%)
  matrix products  25 us (2%)
    ppermute x162, starting transfers between devices, send(): return lax.ppermute(values, ('section', 'dp'), pairs)  312 us
    dynamic_update_slice x12, local copies, waits for them, and re-layouts, gather_long(): lax.dynamic_update_index_in_dim(full, jnp.where(inside, running, current)...  208 us
    pallas_call x10, Pallas kernels, run(): pl.pallas_call(kernel, out_shape=tuple(outs), in_specs=[whole] * len(args...  107 us
    ppermute x162, waiting for transfers between devices, send(): return lax.ppermute(values, ('section', 'dp'), pairs)  78.1 us
    ppermute x23, starting transfers between devices, swap(): return lax.ppermute(values, axis, [(0, 1), (1, 0)])  64.6 us
    dynamic_slice x73, local copies, waits for them, and re-layouts, pick(): return lax.dynamic_index_in_dim(values, index, 0, keepdims=False)  57.5 us
    unnamed x193, local copies, waits for them, and re-layouts  44 us
    pallas_call x2, Pallas kernels, feed_forward(): pl.pallas_call(feed_forward_kernel, grid=(steps,), out_shape=outs, in_spe...  39.2 us
  transfers between devices with their start and end apart: 192, of which 35 were waited for; matrix products, arithmetic and copies ran while one was open for 43% of the time, Pallas kernels for 10%

profile of v1, /device:TPU:0, one launch (start us, length us, event | category | flops | bytes accessed | tf_op | source)
XLA Modules:
  0.0 1274.5 jit_solution(15857768356484209793)
XLA Ops:
  1.1 6.7 collective-permute-start.1
  33.8 15.7 %shard_map.135 = (bf16[256,1024]{1,0:T(8,128)(2,1)}, f32[256,1024]{1,0:T(8,128)}, bf16[256,1024]{1,0:T(8,128)(2,1)}, bf16[1024,1024]{1,0:T(8,128)(2,1)}, bf16[25...) custom-call(bf16[1024,1024]{1,0:T(8,128)(2,1)} %get-tuple-element.19, ...), custom_call_target="tpu_custom_call" | custom-call | flops 3221225472 | bytes 13156352 | tf_op jit(solution)/shard_map/pallas_call | solution.py:361
  51.4 15.5 %shard_map.138 = (bf16[256,1024]{1,0:T(8,128)(2,1)}, f32[256,1024]{1,0:T(8,128)}, bf16[256,1024]{1,0:T(8,128)(2,1)}, bf16[1024,1024]{1,0:T(8,128)(2,1)}, bf16[25...) custom-call(bf16[1024,1024]{1,0:T(8,128)(2,1)} %get-tuple-element.19, ...), custom_call_target="tpu_custom_call" | custom-call | flops 3221225472 | bytes 13156352 | tf_op jit(solution)/shard_map/pallas_call | solution.py:361
  69.7 7.1 shard_map.136
  78.8 14.8 %copy.104 = bf16[1024,2,1408]{0,2,1:T(8,128)(2,1)} copy(bf16[1024,2,1408]{2,1,0:T(2,128)(2,1)} %param.13) | data formatting | bytes 11534336 | tf_op args[5]
  93.7 14.9 %copy.105 = bf16[1024,11,2,128]{3,2,1,0:T(2,128)(2,1)} copy(bf16[1024,11,2,128]{0,3,1,2:T(8,128)(2,1)} %bitcast.937) | data formatting | bytes 11534336 | tf_op jit(solution)/shard_map/transpose | solution.py:647
  108.6 14.0 %reshape.359.w_in = bf16[1024,2816]{1,0:T(8,128)(2,1)} reshape(bf16[1024,11,2,128]{3,2,1,0:T(2,128)(2,1)} %copy.105) | data formatting | bytes 11534336 | tf_op jit(solution)/shard_map/reshape | solution.py:647
  128.9 7.0 shard_map.139
  136.1 19.5 %shard_map.137 = (f32[256,1024]{1,0:T(8,128)}, bf16[256,1024]{1,0:T(8,128)(2,1)}, bf16[256,1408]{1,0:T(8,128)(2,1)}, bf16[256,2816]{1,0:T(8,128)(2,1)}, f32[256,1024]{1,0:T(8,128)}, /*index=5*/bf16[256,1024]{1,0:T(8,128)(2,1)}) custom-call(bf16[256,1024]{1,0:T(8,128)(2,1)} %get-tuple-element.83.latent, bf16[256,1024]{1,0:T(8,128)(2,1)} %get-tuple-element.84.part_in, ...), custom_call_target="tpu_custom_call" | custom-call | flops 4429185024 | bytes 19136512 | tf_op jit(solution)/shard_map/pallas_call | solution.py:432
  159.4 19.7 %shard_map.140 = (f32[256,1024]{1,0:T(8,128)}, bf16[256,1024]{1,0:T(8,128)(2,1)}, bf16[256,1408]{1,0:T(8,128)(2,1)}, bf16[256,2816]{1,0:T(8,128)(2,1)}, f32[256,1024]{1,0:T(8,128)}, /*index=5*/bf16[256,1024]{1,0:T(8,128)(2,1)}) custom-call(bf16[256,1024]{1,0:T(8,128)(2,1)} %get-tuple-element.89.latent, bf16[256,1024]{1,0:T(8,128)(2,1)} %get-tuple-element.90.part_in, ...), custom_call_target="tpu_custom_call" | custom-call | flops 4429185024 | bytes 19136512 | tf_op jit(solution)/shard_map/pallas_call | solution.py:432
  209.0 9.5 shard_map.141
  220.2 9.5 shard_map.144
  233.1 7.8 collective-permute-start.103
  246.2 15.4 %shard_map.142 = (bf16[256,1024]{1,0:T(8,128)(2,1)}, bf16[256,512]{1,0:T(8,128)(2,1)}, bf16[1024,512]{1,0:T(8,128)(2,1)}, bf16[1024,512]{1,0:T(8,128)(2,1)}, bf1...) custom-call(bf16[256,1024]{1,0:T(8,128)(2,1)} %get-tuple-element.83.latent, ...), custom_call_target="tpu_custom_call" | custom-call | flops 3221225472 | bytes 17895424 | tf_op jit(solution)/shard_map/pallas_call | solution.py:361
  263.8 15.1 %shard_map.145 = (bf16[256,1024]{1,0:T(8,128)(2,1)}, bf16[256,512]{1,0:T(8,128)(2,1)}, bf16[1024,512]{1,0:T(8,128)(2,1)}, bf16[1024,512]{1,0:T(8,128)(2,1)}, bf1...) custom-call(bf16[256,1024]{1,0:T(8,128)(2,1)} %get-tuple-element.89.latent, ...), custom_call_target="tpu_custom_call" | custom-call | flops 3221225472 | bytes 17895424 | tf_op jit(solution)/shard_map/pallas_call | solution.py:361
  290.3 15.4 %collective-permute-done.131 = f32[4,1024]{1,0:T(4,128)S(1)} collective-permute-done((f32[4,1024]{1,0:T(4,128)S(1)}, f32[4,1024]{1,0:T(4,128)S(1)}, u32[]{:S(2)}, u32[]{:S(2)}) %collective-permute-start.131) | collective-permute-done | bytes 16416 | tf_op jit(solution)/shard_map/ppermute | solution.py:516
  326.1 6.5 collective-permute-start.75
  358.0 7.7 collective-permute-start.179
  390.8 20.1 %collective-permute-start.17 = (bf16[512,1024]{1,0:T(8,128)(2,1)}, bf16[512,1024]{1,0:T(8,128)(2,1)}, u32[]{:S(2)}, u32[]{:S(2)}) collective-permute-start(bf16[512,1024]{1,0:T(8,128)(2,1)} %get-tuple-element.209), channel_id=1, source_target_pairs={{0,8},{8,0},{1,9},{9,1},{2,10},{10,2},{3,11},{11,3},{4,12},{12,4},... | collective-permute-start | bytes 3145736 | tf_op jit(solution)/shard_map/ppermute | solution.py:516
  417.6 9.3 collective-permute-start.47
  439.9 8.4 collective-permute-done.16.query_got
  479.9 8.2 collective-permute-start.172
  535.3 9.3 collective-permute-start.92
  559.3 9.2 collective-permute-done.99
  626.0 9.4 collective-permute-start.139
  715.7 14.3 %collective-permute-done.161 = bf16[32,2816]{1,0:T(8,128)(2,1)S(1)} collective-permute-done((bf16[32,2816]{1,0:T(8,128)(2,1)S(1)}, bf16[32,2816]{1,0:T(8,128)(2,1)S(1)}, u32[]{:S(2)}, u32[]{:S(2)}) %collective-permute-start.161) | collective-permute-done | bytes 180256 | tf_op jit(solution)/shard_map/ppermute | solution.py:540
  754.6 9.5 collective-permute-start.34
  782.3 17.8 %dynamic_update_slice.274 = bf16[4,128,1536]{1,0,2:T(4,128)(2,1)S(1)} dynamic-update-slice(bf16[4,128,1536]{1,0,2:T(4,128)(2,1)S(1)} %broadcast.36.clone.1, bf16[1,128,1536]{1,0,2:T(2,128)(2,1)} %copy.135, s32[]{:T(128)S(6)} %select_n.1253, s32[]{:T(128)} %constant.999.clone.1, s32[]{:T(128)} %constant.999.clone.1) | dynamic-update-slice | bytes 786436 | tf_op jit(solution)/shard_map/jit(dynamic_update_index_in_dim)/dynamic_update_slice | solution.py:566
  806.3 6.2 collective-permute-start.35
  816.0 6.9 collective-permute-start.71
  846.4 10.9 convert_bitcast_fusion.1
  857.3 9.6 copy.154
  866.9 9.6 copy.156
  907.9 16.7 %dynamic_update_slice.275 = bf16[4,128,1536]{1,0,2:T(4,128)(2,1)S(1)} dynamic-update-slice(bf16[4,128,1536]{1,0,2:T(4,128)(2,1)S(1)} %dynamic_update_slice.274, bf16[1,128,1536]{1,0,2:T(2,128)(2,1)S(1)} %copy.137, s32[]{:T(128)S(6)} %select_n.1255, s32[]{:T(128)} %constant.999.clone.1, s32[]{:T(128)} %constant.999.clone.1) | dynamic-update-slice | bytes 786436 | tf_op jit(solution)/shard_map/jit(dynamic_update_index_in_dim)/dynamic_update_slice | solution.py:576
  933.3 17.8 %dynamic_update_slice.260 = bf16[4,128,1536]{1,0,2:T(4,128)(2,1)S(1)} dynamic-update-slice(bf16[4,128,1536]{1,0,2:T(4,128)(2,1)S(1)} %broadcast.36.clone, bf16[1,128,1536]{1,0,2:T(2,128)(2,1)} %copy.118, s32[]{:T(128)S(6)} %select_n.1253, s32[]{:T(128)} %constant.999.clone.1, s32[]{:T(128)} %constant.999.clone.1) | dynamic-update-slice | bytes 786436 | tf_op jit(solution)/shard_map/jit(dynamic_update_index_in_dim)/dynamic_update_slice | solution.py:566
  959.7 9.0 collective-permute-start.27
  977.5 17.8 %dynamic_update_slice.276 = bf16[4,128,1536]{1,0,2:T(4,128)(2,1)S(1)} dynamic-update-slice(bf16[4,128,1536]{1,0,2:T(4,128)(2,1)S(1)} %dynamic_update_slice.275, bf16[1,128,1536]{1,0,2:T(2,128)(2,1)} %copy.139, s32[]{:T(128)S(6)} %select_n.1257, s32[]{:T(128)} %constant.999.clone.1, s32[]{:T(128)} %constant.999.clone.1) | dynamic-update-slice | bytes 786436 | tf_op jit(solution)/shard_map/jit(dynamic_update_index_in_dim)/dynamic_update_slice | solution.py:576
  1021.3 17.8 %dynamic_update_slice.261 = bf16[4,128,1536]{1,0,2:T(4,128)(2,1)S(1)} dynamic-update-slice(bf16[4,128,1536]{1,0,2:T(4,128)(2,1)S(1)} %dynamic_update_slice.260, bf16[1,128,1536]{1,0,2:T(2,128)(2,1)} %copy.120, s32[]{:T(128)S(6)} %select_n.1255, s32[]{:T(128)} %constant.999.clone.1, s32[]{:T(128)} %constant.999.clone.1) | dynamic-update-slice | bytes 786436 | tf_op jit(solution)/shard_map/jit(dynamic_update_index_in_dim)/dynamic_update_slice | solution.py:576
  1049.4 17.8 %dynamic_update_slice.277 = bf16[4,128,1536]{1,0,2:T(4,128)(2,1)S(1)} dynamic-update-slice(bf16[4,128,1536]{1,0,2:T(4,128)(2,1)S(1)} %dynamic_update_slice.276, bf16[1,128,1536]{1,0,2:T(2,128)(2,1)} %copy.141, s32[]{:T(128)S(6)} %select_n.1259, s32[]{:T(128)} %constant.999.clone.1, s32[]{:T(128)} %constant.999.clone.1) | dynamic-update-slice | bytes 786436 | tf_op jit(solution)/shard_map/jit(dynamic_update_index_in_dim)/dynamic_update_slice | solution.py:576
  1075.7 17.8 %dynamic_update_slice.278 = bf16[4,128,1536]{1,0,2:T(4,128)(2,1)S(1)} dynamic-update-slice(bf16[4,128,1536]{1,0,2:T(4,128)(2,1)S(1)} %dynamic_update_slice.277, bf16[1,128,1536]{1,0,2:T(2,128)(2,1)} %copy.143, s32[]{:T(128)S(6)} %select_n.1261, s32[]{:T(128)} %constant.999.clone.1, s32[]{:T(128)} %constant.999.clone.1) | dynamic-update-slice | bytes 786436 | tf_op jit(solution)/shard_map/jit(dynamic_update_index_in_dim)/dynamic_update_slice | solution.py:576
  1102.1 17.8 %dynamic_update_slice.279 = bf16[4,128,1536]{1,0,2:T(4,128)(2,1)S(1)} dynamic-update-slice(bf16[4,128,1536]{1,0,2:T(4,128)(2,1)S(1)} %dynamic_update_slice.278, bf16[1,128,1536]{1,0,2:T(2,128)(2,1)} %copy.145, s32[]{:T(128)S(6)} %select_n.1263, s32[]{:T(128)} %constant.999.clone.1, s32[]{:T(128)} %constant.999.clone.1) | dynamic-update-slice | bytes 786436 | tf_op jit(solution)/shard_map/jit(dynamic_update_index_in_dim)/dynamic_update_slice | solution.py:576
  1134.8 17.9 %dynamic_update_slice.280 = bf16[4,128,1536]{1,0,2:T(4,128)(2,1)S(1)} dynamic-update-slice(bf16[4,128,1536]{1,0,2:T(4,128)(2,1)S(1)} %dynamic_update_slice.279, bf16[1,128,1536]{1,0,2:T(2,128)(2,1)} %copy.147, s32[]{:T(128)S(6)} %select_n.1265, s32[]{:T(128)} %constant.999.clone.1, s32[]{:T(128)} %constant.999.clone.1) | dynamic-update-slice | bytes 786436 | tf_op jit(solution)/shard_map/jit(dynamic_update_index_in_dim)/dynamic_update_slice | solution.py:576
  1155.3 16.7 %dynamic_update_slice.262 = bf16[4,128,1536]{1,0,2:T(4,128)(2,1)S(1)} dynamic-update-slice(bf16[4,128,1536]{1,0,2:T(4,128)(2,1)S(1)} %dynamic_update_slice.261, bf16[1,128,1536]{1,0,2:T(2,128)(2,1)S(1)} %copy.122, s32[]{:T(128)S(6)} %select_n.1257, s32[]{:T(128)} %constant.999.clone.1, s32[]{:T(128)} %constant.999.clone.1) | dynamic-update-slice | bytes 786436 | tf_op jit(solution)/shard_map/jit(dynamic_update_index_in_dim)/dynamic_update_slice | solution.py:576
  1182.6 16.7 %dynamic_update_slice.263 = bf16[4,128,1536]{1,0,2:T(4,128)(2,1)S(1)} dynamic-update-slice(bf16[4,128,1536]{1,0,2:T(4,128)(2,1)S(1)} %dynamic_update_slice.262, bf16[1,128,1536]{1,0,2:T(2,128)(2,1)S(1)} %copy.124, s32[]{:T(128)S(6)} %select_n.1259, s32[]{:T(128)} %constant.999.clone.1, s32[]{:T(128)} %constant.999.clone.1) | dynamic-update-slice | bytes 786436 | tf_op jit(solution)/shard_map/jit(dynamic_update_index_in_dim)/dynamic_update_slice | solution.py:576
  1202.3 16.7 %dynamic_update_slice.264 = bf16[4,128,1536]{1,0,2:T(4,128)(2,1)S(1)} dynamic-update-slice(bf16[4,128,1536]{1,0,2:T(4,128)(2,1)S(1)} %dynamic_update_slice.263, bf16[1,128,1536]{1,0,2:T(2,128)(2,1)S(1)} %copy.126, s32[]{:T(128)S(6)} %select_n.1261, s32[]{:T(128)} %constant.999.clone.1, s32[]{:T(128)} %constant.999.clone.1) | dynamic-update-slice | bytes 786436 | tf_op jit(solution)/shard_map/jit(dynamic_update_index_in_dim)/dynamic_update_slice | solution.py:576
  1222.0 16.7 %dynamic_update_slice.265 = bf16[4,128,1536]{1,0,2:T(4,128)(2,1)S(1)} dynamic-update-slice(bf16[4,128,1536]{1,0,2:T(4,128)(2,1)S(1)} %dynamic_update_slice.264, bf16[1,128,1536]{1,0,2:T(2,128)(2,1)S(1)} %copy.128, s32[]{:T(128)S(6)} %select_n.1263, s32[]{:T(128)} %constant.999.clone.1, s32[]{:T(128)} %constant.999.clone.1) | dynamic-update-slice | bytes 786436 | tf_op jit(solution)/shard_map/jit(dynamic_update_index_in_dim)/dynamic_update_slice | solution.py:576
  1242.9 17.9 %dynamic_update_slice.266 = bf16[4,128,1536]{1,0,2:T(4,128)(2,1)S(1)} dynamic-update-slice(bf16[4,128,1536]{1,0,2:T(4,128)(2,1)S(1)} %dynamic_update_slice.265, bf16[1,128,1536]{1,0,2:T(2,128)(2,1)} %copy.130, s32[]{:T(128)S(6)} %select_n.1265, s32[]{:T(128)} %constant.999.clone.1, s32[]{:T(128)} %constant.999.clone.1) | dynamic-update-slice | bytes 786436 | tf_op jit(solution)/shard_map/jit(dynamic_update_index_in_dim)/dynamic_update_slice | solution.py:576
  1267.6 6.6 copy.155
  (880 shorter events, 646.9 us)
Async XLA Ops:
  0.6 31.0 %collective-permute-start = (bf16[3,1024,512]{2,1,0:T(8,128)(2,1)}, bf16[3,1024,512]{2,1,0:T(8,128)(2,1)S(1)}, u32[]{:S(2)}, u32[]{:S(2)}) collective-permute-start(bf16[3,1024,512]{2,1,0:T(8,128)(2,1)} %bitcast.993), channel_id=1, source_target_pairs={{0,16},{16,0},{1,17},{17,1},{2,18},{18,2},{3,19},{19,3},{4,20},{20... | collective-permute-start | bytes 9437192 | tf_op jit(solution)/shard_map/ppermute | solution.py:516
  67.0 61.2 %collective-permute-start.6 = (bf16[256,1024]{1,0:T(8,128)(2,1)}, bf16[256,1024]{1,0:T(8,128)(2,1)S(1)}, u32[]{:S(2)}, u32[]{:S(2)}) collective-permute-start(bf16[256,1024]{1,0:T(8,128)(2,1)} %get-tuple-element.88.part_in), channel_id=1, source_target_pairs={{0,8},{8,0},{1,9},{9,1},{2,10},{10,2},{3,11},{11,3},{4,12},{12,4},... | collective-permute-start | bytes 1572872 | tf_op jit(solution)/shard_map/ppermute | solution.py:516
  76.8 59.3 %collective-permute-start.4 = (bf16[256,1024]{1,0:T(8,128)(2,1)}, bf16[256,1024]{1,0:T(8,128)(2,1)}, u32[]{:S(2)}, u32[]{:S(2)}) collective-permute-start(bf16[256,1024]{1,0:T(8,128)(2,1)} %get-tuple-element.84.part_in), channel_id=1, source_target_pairs={{0,8},{8,0},{1,9},{9,1},{2,10},{10,2},{3,11},{11,3},{4,12},{12,4},... | collective-permute-start | bytes 1572872 | tf_op jit(solution)/shard_map/ppermute | solution.py:516
  156.7 50.7 %collective-permute-start.5 = (bf16[256,512]{1,0:T(8,128)(2,1)S(1)}, bf16[256,512]{1,0:T(8,128)(2,1)S(1)}, u32[]{:S(2)}, u32[]{:S(2)}) collective-permute-start(bf16[256,512]{1,0:T(8,128)(2,1)S(1)} %dynamic-slice_convert_fusion.1), channel_id=1, source_target_pairs={{0,8},{8,0},{1,9},{9,1},{2,10},{10,2},{3,11},{11,3},{4,12},{12,4},... | collective-permute-start | bytes 786440 | tf_op jit(solution)/shard_map/ppermute | solution.py:516
  186.2 34.0 %collective-permute-start.14 = (bf16[256,1024]{1,0:T(8,128)(2,1)}, bf16[256,1024]{1,0:T(8,128)(2,1)}, u32[]{:S(2)}, u32[]{:S(2)}) collective-permute-start(bf16[256,1024]{1,0:T(8,128)(2,1)} %get-tuple-element.107.inner_part), channel_id=1, source_target_pairs={{0,8},{8,0},{1,9},{9,1},{2,10},{10,2},{3,11},{11,3},{4,12},{12,4},... | collective-permute-start | bytes 1572872 | tf_op jit(solution)/shard_map/ppermute | solution.py:516
  201.5 131.7 %collective-permute-start.164 = (bf16[1408,512]{1,0:T(8,128)(2,1)}, bf16[1408,512]{1,0:T(8,128)(2,1)}, u32[]{:S(2)}, u32[]{:S(2)}) collective-permute-start(bf16[1408,512]{1,0:T(8,128)(2,1)} %convolution_convert_fusion.3), channel_id=1, source_target_pairs={{0,16},{16,0},{1,17},{17,1},{2,18},{18,2},{3,19},{19,3},{4,20},{20... | collective-permute-start | bytes 4325384 | tf_op jit(solution)/shard_map/ppermute | solution.py:516
  207.8 36.7 %collective-permute-start.9 = (bf16[2,128,512]{2,1,0:T(8,128)(2,1)S(1)}, bf16[2,128,512]{2,1,0:T(8,128)(2,1)S(1)}, u32[]{:S(2)}, u32[]{:S(2)}) collective-permute-start(bf16[2,128,512]{2,1,0:T(8,128)(2,1)S(1)} %get-tuple-element.290), channel_id=1, source_target_pairs={{0,16},{16,0},{1,17},{17,1},{2,18},{18,2},{3,19},{19,3},{4,20},{20... | collective-permute-start | bytes 786440 | tf_op jit(solution)/shard_map/ppermute | solution.py:516
  229.7 33.3 %collective-permute-start.15 = (bf16[256,1024]{1,0:T(8,128)(2,1)}, bf16[256,1024]{1,0:T(8,128)(2,1)S(1)}, u32[]{:S(2)}, u32[]{:S(2)}) collective-permute-start(bf16[256,1024]{1,0:T(8,128)(2,1)} %get-tuple-element.113.normed_part), channel_id=1, source_target_pairs={{0,8},{8,0},{1,9},{9,1},{2,10},{10,2},{3,11},{11,3},{4,12},{12,4},... | collective-permute-start | bytes 1572872 | tf_op jit(solution)/shard_map/ppermute | solution.py:516
  233.1 107.9 %collective-permute-start.103 = (bf16[512,1024]{1,0:T(8,128)(2,1)}, bf16[512,1024]{1,0:T(8,128)(2,1)}, u32[]{:S(2)}, u32[]{:S(2)}) collective-permute-start(bf16[512,1024]{1,0:T(8,128)(2,1)} %convolution_convert_fusion.5), channel_id=1, source_target_pairs={{0,16},{1,17},{2,18},{3,19},{4,20},{5,21},{6,22},{7,23},{8,24},{9,... | collective-permute-start | bytes 3145736 | tf_op jit(solution)/shard_map/ppermute | solution.py:701
  281.5 145.4 %collective-permute-start.13 = (bf16[512,1024]{1,0:T(8,128)(2,1)S(1)}, bf16[512,1024]{1,0:T(8,128)(2,1)S(1)}, u32[]{:S(2)}, u32[]{:S(2)}) collective-permute-start(bf16[512,1024]{1,0:T(8,128)(2,1)S(1)} %get-tuple-element.211), channel_id=1, source_target_pairs={{0,8},{8,0},{1,9},{9,1},{2,10},{10,2},{3,11},{11,3},{4,12},{12,4},... | collective-permute-start | bytes 3145736 | tf_op jit(solution)/shard_map/ppermute | solution.py:516
  326.1 109.6 %collective-permute-start.75 = (bf16[512,1024]{1,0:T(8,128)(2,1)}, bf16[512,1024]{1,0:T(8,128)(2,1)}, u32[]{:S(2)}, u32[]{:S(2)}) collective-permute-start(bf16[512,1024]{1,0:T(8,128)(2,1)} %convolution_convert_fusion.6), channel_id=1, source_target_pairs={{16,0},{17,1},{18,2},{19,3},{20,4},{21,5},{22,6},{23,7},{24,8},{25... | collective-permute-start | bytes 3145736 | tf_op jit(solution)/shard_map/ppermute | solution.py:701
  390.8 58.5 %collective-permute-start.17 = (bf16[512,1024]{1,0:T(8,128)(2,1)}, bf16[512,1024]{1,0:T(8,128)(2,1)}, u32[]{:S(2)}, u32[]{:S(2)}) collective-permute-start(bf16[512,1024]{1,0:T(8,128)(2,1)} %get-tuple-element.209), channel_id=1, source_target_pairs={{0,8},{8,0},{1,9},{9,1},{2,10},{10,2},{3,11},{11,3},{4,12},{12,4},... | collective-permute-start | bytes 3145736 | tf_op jit(solution)/shard_map/ppermute | solution.py:516
  416.9 180.3 %collective-permute-start.136 = (bf16[512,2816]{1,0:T(8,128)(2,1)}, bf16[512,2816]{1,0:T(8,128)(2,1)}, u32[]{:S(2)}, u32[]{:S(2)}) collective-permute-start(bf16[512,2816]{1,0:T(8,128)(2,1)} %convolution_convert_fusion), channel_id=1, source_target_pairs={{0,16},{16,0},{1,17},{17,1},{2,18},{18,2},{3,19},{19,3},{4,20},{20... | collective-permute-start | bytes 8650760 | tf_op jit(solution)/shard_map/ppermute | solution.py:516
  417.6 222.2 %collective-permute-start.47 = (bf16[1024,1536]{1,0:T(8,128)(2,1)}, bf16[1024,1536]{1,0:T(8,128)(2,1)}, u32[]{:S(2)}, u32[]{:S(2)}) collective-permute-start(bf16[1024,1536]{1,0:T(8,128)(2,1)} %convolution_convert_fusion.2), channel_id=1, source_target_pairs={{0,16},{1,17},{2,18},{3,19},{4,20},{5,21},{6,22},{7,23},{8,24},{9,... | collective-permute-start | bytes 9437192 | tf_op jit(solution)/shard_map/ppermute | solution.py:701
  568.6 105.4 %collective-permute-start.19 = (bf16[1024,1536]{0,1:T(8,128)(2,1)S(1)}, bf16[1024,1536]{0,1:T(8,128)(2,1)S(1)}, u32[]{:S(2)}, u32[]{:S(2)}) collective-permute-start(bf16[1024,1536]{0,1:T(8,128)(2,1)S(1)} %copy-done.14), channel_id=1, source_target_pairs={{16,0},{17,1},{18,2},{19,3},{20,4},{21,5},{22,6},{23,7},{24,8},{25... | collective-permute-start | bytes 9437192 | tf_op jit(solution)/shard_map/ppermute | solution.py:701
  645.5 48.1 %collective-permute-start.61 = (bf16[256,1536]{1,0:T(8,128)(2,1)}, bf16[256,1536]{1,0:T(8,128)(2,1)}, u32[]{:S(2)}, u32[]{:S(2)}) collective-permute-start(bf16[256,1536]{1,0:T(8,128)(2,1)} %dynamic-slice_bitcast_fusion.4), channel_id=1, source_target_pairs={{16,17},{17,16},{18,19},{19,18},{20,21},{21,20},{22,23},{23,22},{2... | collective-permute-start | bytes 2359304 | tf_op jit(solution)/shard_map/ppermute | solution.py:540
  656.6 29.8 %collective-permute-start.143 = (bf16[64,2816]{1,0:T(8,128)(2,1)S(1)}, bf16[64,2816]{1,0:T(8,128)(2,1)}, u32[]{:S(2)}, u32[]{:S(2)}) collective-permute-start(bf16[64,2816]{1,0:T(8,128)(2,1)S(1)} %add_convert_fusion.10), channel_id=1, source_target_pairs={{0,1},{1,0},{2,3},{3,2},{4,5},{5,4},{6,7},{7,6},{16,17},{17,16},{1... | collective-permute-start | bytes 1081352 | tf_op jit(solution)/shard_map/ppermute | solution.py:540
  667.6 32.8 %collective-permute-start.49 = (bf16[128,1536]{1,0:T(8,128)(2,1)}, bf16[128,1536]{1,0:T(8,128)(2,1)}, u32[]{:S(2)}, u32[]{:S(2)}) collective-permute-start(bf16[128,1536]{1,0:T(8,128)(2,1)} %get-tuple-element.219), channel_id=1, source_target_pairs={{16,18},{17,19},{18,20},{19,21},{24,26},{25,27},{26,28},{27,29}} | collective-permute-start | bytes 1179656 | tf_op jit(solution)/shard_map/ppermute | solution.py:540
  669.2 31.9 %collective-permute-start.52 = (bf16[128,1536]{1,0:T(8,128)(2,1)}, bf16[128,1536]{1,0:T(8,128)(2,1)}, u32[]{:S(2)}, u32[]{:S(2)}) collective-permute-start(bf16[128,1536]{1,0:T(8,128)(2,1)} %get-tuple-element.220), channel_id=1, source_target_pairs={{20,18},{21,19},{22,20},{23,21},{28,26},{29,27},{30,28},{31,29}} | collective-permute-start | bytes 1179656 | tf_op jit(solution)/shard_map/ppermute | solution.py:540
  689.2 59.0 %collective-permute-start.33 = (bf16[256,1536]{1,0:T(8,128)(2,1)S(1)}, bf16[256,1536]{1,0:T(8,128)(2,1)S(1)}, u32[]{:S(2)}, u32[]{:S(2)}) collective-permute-start(bf16[256,1536]{1,0:T(8,128)(2,1)S(1)} %copy-done.39), channel_id=1, source_target_pairs={{0,1},{1,0},{2,3},{3,2},{4,5},{5,4},{6,7},{7,6},{8,9},{9,8},{10,11... | collective-permute-start | bytes 2359304 | tf_op jit(solution)/shard_map/ppermute | solution.py:540
  712.3 32.3 %collective-permute-start.147 = (bf16[64,2816]{1,0:T(8,128)(2,1)S(1)}, bf16[64,2816]{1,0:T(8,128)(2,1)S(1)}, u32[]{:S(2)}, u32[]{:S(2)}) collective-permute-start(bf16[64,2816]{1,0:T(8,128)(2,1)S(1)} %get-tuple-element.174), channel_id=1, source_target_pairs={{2,0},{3,1},{4,2},{5,3},{6,4},{7,5},{18,16},{19,17},{20,18},{21,19... | collective-permute-start | bytes 1081352 | tf_op jit(solution)/shard_map/ppermute | solution.py:540
  714.9 30.4 %collective-permute-start.53 = (bf16[128,1536]{1,0:T(8,128)(2,1)S(1)}, bf16[128,1536]{1,0:T(8,128)(2,1)S(1)}, u32[]{:S(2)}, u32[]{:S(2)}) collective-permute-start(bf16[128,1536]{1,0:T(8,128)(2,1)S(1)} %get-tuple-element.218), channel_id=1, source_target_pairs={{18,16},{19,17},{20,18},{21,19},{22,20},{23,21},{26,24},{27,25},{2... | collective-permute-start | bytes 1179656 | tf_op jit(solution)/shard_map/ppermute | solution.py:540
  746.8 29.8 %collective-permute-start.148 = (bf16[64,2816]{1,0:T(8,128)(2,1)S(1)}, bf16[64,2816]{1,0:T(8,128)(2,1)}, u32[]{:S(2)}, u32[]{:S(2)}) collective-permute-start(bf16[64,2816]{1,0:T(8,128)(2,1)S(1)} %collective-permute-done.147), channel_id=1, source_target_pairs={{2,0},{3,1},{4,2},{5,3},{18,16},{19,17},{20,18},{21,19},{10,8},{11... | collective-permute-start | bytes 1081352 | tf_op jit(solution)/shard_map/ppermute | solution.py:540
  748.2 84.9 %collective-permute-start.163 = (bf16[128,2816]{1,0:T(8,128)(2,1)}, bf16[128,2816]{1,0:T(8,128)(2,1)}, u32[]{:S(2)}, u32[]{:S(2)}) collective-permute-start(bf16[128,2816]{1,0:T(8,128)(2,1)} %bitcast.267), channel_id=1, source_target_pairs={{0,1},{1,0},{2,3},{3,2},{4,5},{5,4},{6,7},{7,6},{16,17},{17,16},{1... | collective-permute-start | bytes 2162696 | tf_op jit(solution)/shard_map/ppermute | solution.py:540
  767.6 38.8 %collective-permute-start.25 = (bf16[128,1536]{1,0:T(8,128)(2,1)}, bf16[128,1536]{1,0:T(8,128)(2,1)}, u32[]{:S(2)}, u32[]{:S(2)}) collective-permute-start(bf16[128,1536]{1,0:T(8,128)(2,1)} %get-tuple-element.226), channel_id=1, source_target_pairs={{2,0},{3,1},{4,2},{5,3},{6,4},{7,5},{10,8},{11,9},{12,10},{13,11},... | collective-permute-start | bytes 1179656 | tf_op jit(solution)/shard_map/ppermute | solution.py:540
  768.9 43.7 %collective-permute-start.22 = (bf16[128,1536]{1,0:T(8,128)(2,1)}, bf16[128,1536]{1,0:T(8,128)(2,1)}, u32[]{:S(2)}, u32[]{:S(2)}) collective-permute-start(bf16[128,1536]{1,0:T(8,128)(2,1)} %get-tuple-element.225), channel_id=1, source_target_pairs={{0,2},{1,3},{2,4},{3,5},{4,6},{5,7},{8,10},{9,11},{10,12},{11,13},... | collective-permute-start | bytes 1179656 | tf_op jit(solution)/shard_map/ppermute | solution.py:540
  776.6 48.6 %collective-permute-start.146 = (bf16[64,2816]{1,0:T(8,128)(2,1)}, bf16[64,2816]{1,0:T(8,128)(2,1)}, u32[]{:S(2)}, u32[]{:S(2)}) collective-permute-start(bf16[64,2816]{1,0:T(8,128)(2,1)} %collective-permute-done.145), channel_id=1, source_target_pairs={{4,6},{5,7},{20,22},{21,23},{12,14},{13,15},{28,30},{29,31}} | collective-permute-start | bytes 1081352 | tf_op jit(solution)/shard_map/ppermute | solution.py:540
  778.1 51.4 %collective-permute-start.149 = (bf16[64,2816]{1,0:T(8,128)(2,1)}, bf16[64,2816]{1,0:T(8,128)(2,1)}, u32[]{:S(2)}, u32[]{:S(2)}) collective-permute-start(bf16[64,2816]{1,0:T(8,128)(2,1)} %collective-permute-done.148), channel_id=1, source_target_pairs={{2,0},{3,1},{18,16},{19,17},{10,8},{11,9},{26,24},{27,25}} | collective-permute-start | bytes 1081352 | tf_op jit(solution)/shard_map/ppermute | solution.py:540
  822.9 80.5 %collective-permute-start.55 = (bf16[128,1536]{1,0:T(8,128)(2,1)S(1)}, bf16[128,1536]{1,0:T(8,128)(2,1)}, u32[]{:S(2)}, u32[]{:S(2)}) collective-permute-start(bf16[128,1536]{1,0:T(8,128)(2,1)S(1)} %add_convert_fusion.5), channel_id=1, source_target_pairs={{16,18},{17,19},{18,20},{19,21},{20,22},{21,23},{24,26},{25,27},{2... | collective-permute-start | bytes 1179656 | tf_op jit(solution)/shard_map/ppermute | solution.py:540
  825.2 101.9 %collective-permute-start.58 = (bf16[128,1536]{1,0:T(8,128)(2,1)S(1)}, bf16[128,1536]{1,0:T(8,128)(2,1)}, u32[]{:S(2)}, u32[]{:S(2)}) collective-permute-start(bf16[128,1536]{1,0:T(8,128)(2,1)S(1)} %add_convert_fusion.5), channel_id=1, source_target_pairs={{18,16},{19,17},{20,18},{21,19},{22,20},{23,21},{26,24},{27,25},{2... | collective-permute-start | bytes 1179656 | tf_op jit(solution)/shard_map/ppermute | solution.py:540
  828.1 48.4 %collective-permute-start.69 = (bf16[64,1536]{1,0:T(8,128)(2,1)}, bf16[64,1536]{1,0:T(8,128)(2,1)}, u32[]{:S(2)}, u32[]{:S(2)}) collective-permute-start(bf16[64,1536]{1,0:T(8,128)(2,1)} %collective-permute-done.68), channel_id=1, source_target_pairs={{18,20},{19,21},{20,22},{21,23},{26,28},{27,29},{28,30},{29,31}} | collective-permute-start | bytes 589832 | tf_op jit(solution)/shard_map/ppermute | solution.py:540
  829.5 53.3 %collective-permute-start.72 = (bf16[64,1536]{1,0:T(8,128)(2,1)}, bf16[64,1536]{1,0:T(8,128)(2,1)}, u32[]{:S(2)}, u32[]{:S(2)}) collective-permute-start(bf16[64,1536]{1,0:T(8,128)(2,1)} %collective-permute-done.71), channel_id=1, source_target_pairs={{18,16},{19,17},{20,18},{21,19},{26,24},{27,25},{28,26},{29,27}} | collective-permute-start | bytes 589832 | tf_op jit(solution)/shard_map/ppermute | solution.py:540
  833.2 53.4 %collective-permute-start.39 = (bf16[64,1536]{1,0:T(8,128)(2,1)}, bf16[64,1536]{1,0:T(8,128)(2,1)}, u32[]{:S(2)}, u32[]{:S(2)}) collective-permute-start(bf16[64,1536]{1,0:T(8,128)(2,1)} %get-tuple-element.254), channel_id=1, source_target_pairs={{2,0},{3,1},{4,2},{5,3},{6,4},{7,5},{10,8},{11,9},{12,10},{13,11},... | collective-permute-start | bytes 589832 | tf_op jit(solution)/shard_map/ppermute | solution.py:540
  882.8 45.8 %collective-permute-start.26 = (bf16[128,1536]{1,0:T(8,128)(2,1)S(1)}, bf16[128,1536]{1,0:T(8,128)(2,1)}, u32[]{:S(2)}, u32[]{:S(2)}) collective-permute-start(bf16[128,1536]{1,0:T(8,128)(2,1)S(1)} %copy-done.27), channel_id=1, source_target_pairs={{0,1},{1,0},{2,3},{3,2},{4,5},{5,4},{6,7},{7,6},{8,9},{9,8},{10,11... | collective-permute-start | bytes 1179656 | tf_op jit(solution)/shard_map/ppermute | solution.py:540
  891.4 64.2 %collective-permute-start.40 = (bf16[64,1536]{1,0:T(8,128)(2,1)}, bf16[64,1536]{1,0:T(8,128)(2,1)}, u32[]{:S(2)}, u32[]{:S(2)}) collective-permute-start(bf16[64,1536]{1,0:T(8,128)(2,1)} %get-tuple-element.188), channel_id=1, source_target_pairs={{0,2},{1,3},{2,4},{3,5},{4,6},{5,7},{8,10},{9,11},{10,12},{11,13},... | collective-permute-start | bytes 589832 | tf_op jit(solution)/shard_map/ppermute | solution.py:540
  901.4 58.3 %collective-permute-start.43 = (bf16[64,1536]{1,0:T(8,128)(2,1)}, bf16[64,1536]{1,0:T(8,128)(2,1)}, u32[]{:S(2)}, u32[]{:S(2)}) collective-permute-start(bf16[64,1536]{1,0:T(8,128)(2,1)} %get-tuple-element.188), channel_id=1, source_target_pairs={{2,0},{3,1},{4,2},{5,3},{6,4},{7,5},{10,8},{11,9},{12,10},{13,11},... | collective-permute-start | bytes 589832 | tf_op jit(solution)/shard_map/ppermute | solution.py:540
  903.4 220.3 %collective-permute-start.74 = (bf16[256,1536]{1,0:T(8,128)(2,1)}, bf16[256,1536]{1,0:T(8,128)(2,1)}, u32[]{:S(2)}, u32[]{:S(2)}) collective-permute-start(bf16[256,1536]{1,0:T(8,128)(2,1)} %bitcast.118), channel_id=1, source_target_pairs={{16,17},{17,16},{18,19},{19,18},{20,21},{21,20},{22,23},{23,22},{2... | collective-permute-start | bytes 2359304 | tf_op jit(solution)/shard_map/ppermute | solution.py:540
  927.1 45.3 %collective-permute-start.56 = (bf16[128,1536]{1,0:T(8,128)(2,1)}, bf16[128,1536]{1,0:T(8,128)(2,1)}, u32[]{:S(2)}, u32[]{:S(2)}) collective-permute-start(bf16[128,1536]{1,0:T(8,128)(2,1)} %collective-permute-done.55), channel_id=1, source_target_pairs={{18,20},{19,21},{20,22},{21,23},{26,28},{27,29},{28,30},{29,31}} | collective-permute-start | bytes 1179656 | tf_op jit(solution)/shard_map/ppermute | solution.py:540
  928.6 81.8 %collective-permute-start.59 = (bf16[128,1536]{1,0:T(8,128)(2,1)}, bf16[128,1536]{1,0:T(8,128)(2,1)}, u32[]{:S(2)}, u32[]{:S(2)}) collective-permute-start(bf16[128,1536]{1,0:T(8,128)(2,1)} %collective-permute-done.58), channel_id=1, source_target_pairs={{18,16},{19,17},{20,18},{21,19},{26,24},{27,25},{28,26},{29,27}} | collective-permute-start | bytes 1179656 | tf_op jit(solution)/shard_map/ppermute | solution.py:540
  959.7 55.3 %collective-permute-start.27 = (bf16[128,1536]{1,0:T(8,128)(2,1)S(1)}, bf16[128,1536]{1,0:T(8,128)(2,1)}, u32[]{:S(2)}, u32[]{:S(2)}) collective-permute-start(bf16[128,1536]{1,0:T(8,128)(2,1)S(1)} %add_convert_fusion.7), channel_id=1, source_target_pairs={{0,2},{1,3},{2,4},{3,5},{4,6},{5,7},{8,10},{9,11},{10,12},{11,13},... | collective-permute-start | bytes 1179656 | tf_op jit(solution)/shard_map/ppermute | solution.py:540
  968.8 31.1 %collective-permute-start.44 = (bf16[64,1536]{1,0:T(8,128)(2,1)}, bf16[64,1536]{1,0:T(8,128)(2,1)}, u32[]{:S(2)}, u32[]{:S(2)}) collective-permute-start(bf16[64,1536]{1,0:T(8,128)(2,1)} %collective-permute-done.43), channel_id=1, source_target_pairs={{2,0},{3,1},{4,2},{5,3},{10,8},{11,9},{12,10},{13,11}} | collective-permute-start | bytes 589832 | tf_op jit(solution)/shard_map/ppermute | solution.py:540
  999.8 43.7 %collective-permute-start.30 = (bf16[128,1536]{1,0:T(8,128)(2,1)S(1)}, bf16[128,1536]{1,0:T(8,128)(2,1)}, u32[]{:S(2)}, u32[]{:S(2)}) collective-permute-start(bf16[128,1536]{1,0:T(8,128)(2,1)S(1)} %add_convert_fusion.7), channel_id=1, source_target_pairs={{2,0},{3,1},{4,2},{5,3},{6,4},{7,5},{10,8},{11,9},{12,10},{13,11},... | collective-permute-start | bytes 1179656 | tf_op jit(solution)/shard_map/ppermute | solution.py:540
  1010.4 34.6 %collective-permute-start.57 = (bf16[128,1536]{1,0:T(8,128)(2,1)}, bf16[128,1536]{1,0:T(8,128)(2,1)}, u32[]{:S(2)}, u32[]{:S(2)}) collective-permute-start(bf16[128,1536]{1,0:T(8,128)(2,1)} %collective-permute-done.56), channel_id=1, source_target_pairs={{20,22},{21,23},{28,30},{29,31}} | collective-permute-start | bytes 1179656 | tf_op jit(solution)/shard_map/ppermute | solution.py:540
  1012.9 113.5 %collective-permute-start.60 = (bf16[128,1536]{1,0:T(8,128)(2,1)}, bf16[128,1536]{1,0:T(8,128)(2,1)}, u32[]{:S(2)}, u32[]{:S(2)}) collective-permute-start(bf16[128,1536]{1,0:T(8,128)(2,1)} %collective-permute-done.59), channel_id=1, source_target_pairs={{18,16},{19,17},{26,24},{27,25}} | collective-permute-start | bytes 1179656 | tf_op jit(solution)/shard_map/ppermute | solution.py:540
  1015.0 161.3 %collective-permute-start.46 = (bf16[256,1536]{1,0:T(8,128)(2,1)}, bf16[256,1536]{1,0:T(8,128)(2,1)}, u32[]{:S(2)}, u32[]{:S(2)}) collective-permute-start(bf16[256,1536]{1,0:T(8,128)(2,1)} %bitcast.950), channel_id=1, source_target_pairs={{0,1},{1,0},{2,3},{3,2},{4,5},{5,4},{6,7},{7,6},{8,9},{9,8},{10,11... | collective-permute-start | bytes 2359304 | tf_op jit(solution)/shard_map/ppermute | solution.py:540
  1043.6 111.1 %collective-permute-start.28 = (bf16[128,1536]{1,0:T(8,128)(2,1)}, bf16[128,1536]{1,0:T(8,128)(2,1)}, u32[]{:S(2)}, u32[]{:S(2)}) collective-permute-start(bf16[128,1536]{1,0:T(8,128)(2,1)} %collective-permute-done.27), channel_id=1, source_target_pairs={{2,4},{3,5},{4,6},{5,7},{10,12},{11,13},{12,14},{13,15}} | collective-permute-start | bytes 1179656 | tf_op jit(solution)/shard_map/ppermute | solution.py:540
  1045.0 129.8 %collective-permute-start.31 = (bf16[128,1536]{1,0:T(8,128)(2,1)}, bf16[128,1536]{1,0:T(8,128)(2,1)}, u32[]{:S(2)}, u32[]{:S(2)}) collective-permute-start(bf16[128,1536]{1,0:T(8,128)(2,1)} %collective-permute-done.30), channel_id=1, source_target_pairs={{2,0},{3,1},{4,2},{5,3},{10,8},{11,9},{12,10},{13,11}} | collective-permute-start | bytes 1179656 | tf_op jit(solution)/shard_map/ppermute | solution.py:540
  1174.8 65.2 %collective-permute-start.32 = (bf16[128,1536]{1,0:T(8,128)(2,1)}, bf16[128,1536]{1,0:T(8,128)(2,1)}, u32[]{:S(2)}, u32[]{:S(2)}) collective-permute-start(bf16[128,1536]{1,0:T(8,128)(2,1)} %collective-permute-done.31), channel_id=1, source_target_pairs={{2,0},{3,1},{10,8},{11,9}} | collective-permute-start | bytes 1179656 | tf_op jit(solution)/shard_map/ppermute | solution.py:540
  (237 other events, 2381.2 us)
